TPU v7x, 256 devices: a whole 4x4x8 slice. The times are simulated.
256 devices in a mesh: bead: 8 (over z), space: 32 (over x, y, core).
Axes of the slice: x: 4, y: 4, z: 8, core: 2. Of those that a mesh axis runs over, the one named last changes fastest.
Arguments:
- positions: float32 [16, 3, 196608], P('bead', None, 'space'), may hold values from -0.6 to 8.6, as said below
- momenta: float32 [16, 3, 196608], P('bead', None, 'space'), may hold values from -6 to 6
- thermostat: float32 [16, 4, 3, 196608], P('bead', None, None, 'space'), may hold values from -3 to 3
- atom_types: int32 [196608], P('space'), may hold values from 0 to 127
- masses: float32 [128], replicated, may hold values from 1 to 16
- pair_table: bfloat16 [128, 128], replicated, may hold values from 0.5 to 2, as said below
- tile_pairs: int32 [32, 2, 672], P('space'), may hold values from 0 to 143, as said below
- tile_count: int32 [32], P('space'), may hold values from 336 to 672
- move_rows: int32 [32, 4, 96], P('space'), may hold values from 0 to 6143, as said below
- move_count: int32 [32, 4], P('space'), may hold values from 32 to 96, as said below
Outputs:
- positions_out: float32 [16, 3, 196608], P('bead', None, 'space')
- momenta_out: float32 [16, 3, 196608], P('bead', None, 'space')
- thermo_out: float32 [16, 4, 3, 196608], P('bead', None, None, 'space')
- forces: float32 [16, 3, 196608], P('bead', None, 'space')
- types_out: int32 [196608], P('space')
Inputs may be any that keep to these rules, and one draw needn't show every extreme that they name: `positions`: slot s of a domain belongs to cell c = s // 128 at y index c // 6 and z index c % 6. `pair_table`: Symmetric. `tile_pairs`: row 0 holds a cell of the domain; row 1 a cell of its extended list: cells of the domain below (0 to 47), of the domain (48 to 95), of the domain above (96 to 143). Entries from tile_count on are padding with valid indices. `move_rows`: the rows listed by one domain are distinct over all four classes; entries from the class's count on are padding. `move_count`: column k counts the cycle polymers a domain sends (+1, -1, +2, -2)[k] domains away on the periodic axis. As many go from domain d to d + 1 as from d + 1 to d, and as many from d to d + 2 as from d + 2 to d.
All inputs are finite; a program needn't handle non-finite values.
Results may differ from a plain program's by a relative error of at most 0.0003.
Values sent between devices are 32-bit elements; how exact they have to be, the bound alone decides.
A program may use at most 128 MiB of HBM per device.

v0:
```python
import math

import jax
import jax.numpy as jnp
from jax import lax
from jax.sharding import PartitionSpec as P

NBEADS = 16
CAP = 128
CHAIN = 4


outer_step = 0.2
inner_step = 0.05
thermal = 1.0
chain_mass = 2.0
cycle_freq = 2.0
pair_reach = 0.4
slab_width = 1.0
offsets = (1, -1, 2, -2)
opposite = (1, 0, 3, 2)
tile_block = 56
highest = lax.Precision.HIGHEST


def shifted(shard, axis, by):
    count = lax.axis_size(axis)
    return lax.ppermute(shard, axis, [(i, (i + by) % count) for i in range(count)])


def extended_2(shard, sides, width):
    for axis, dim in sides:
        count, length = (lax.axis_size(axis), shard.shape[dim])
        up = [(i, (i + 1) % count) for i in range(count)]
        down = [(j, i) for i, j in up]
        last = lax.slice_in_dim(shard, length - width, length, axis=dim)
        first = lax.slice_in_dim(shard, 0, width, axis=dim)
        before = lax.ppermute(last, axis, up)
        after = lax.ppermute(first, axis, down)
        shard = jnp.concatenate([before, shard, after], axis=dim)
    return shard


def chain_half(momenta, thermostat, atom_mass):
    half_step = 0.5 * outer_step
    levels = [thermostat[:, rung_index] for rung_index in range(thermostat.shape[1])]
    deepest = len(levels) - 1
    levels[deepest] = (
        levels[deepest]
        + half_step
        * (chain_mass * levels[deepest - 1] * levels[deepest - 1] - thermal)
        / chain_mass
    )
    for rung_index in range(deepest - 1, -1, -1):
        if rung_index == 0:
            driving = (momenta * momenta / atom_mass - thermal) / chain_mass
        else:
            driving = (
                chain_mass * levels[rung_index - 1] * levels[rung_index - 1] - thermal
            ) / chain_mass
        levels[rung_index] = (
            levels[rung_index] * jnp.exp(-levels[rung_index + 1] * half_step) + half_step * driving
        )
    return (momenta * jnp.exp(-levels[0] * half_step), jnp.stack(levels, axis=1))


def cycle_matrices(bead_total):
    mode_ids = jnp.arange(bead_total, dtype=jnp.int32)
    frequency = 2.0 * cycle_freq * jnp.sin(math.pi * mode_ids.astype(jnp.float32) / bead_total)
    rotation = frequency * outer_step
    moving = mode_ids > 0
    safe_freq = jnp.where(moving, frequency, 1.0)
    forward_map = jnp.where(moving, jnp.sin(rotation) / safe_freq, outer_step)
    backward = -frequency * jnp.sin(rotation)
    cosine = jnp.cos(rotation)
    bead_lag = (mode_ids[:, None] - mode_ids[None, :]) % bead_total
    phases = jnp.cos(
        2.0
        * math.pi
        / bead_total
        * (bead_lag[:, :, None] * mode_ids[None, None, :] % bead_total).astype(jnp.float32)
    )

    def circulant(values):
        return jnp.sum(phases * values, axis=2) / bead_total

    return jnp.stack(
        [
            jnp.stack([circulant(cosine), circulant(forward_map)]),
            jnp.stack([circulant(backward), circulant(cosine)]),
        ]
    )


def per_device(
    positions,
    momenta,
    thermostat,
    atom_types,
    masses,
    pair_table,
    tile_pairs,
    tile_count,
    move_rows,
    move_count,
):
    bead_local = positions.shape[0]
    slot_total = positions.shape[2]
    type_total = masses.shape[0]
    type_ids = jnp.arange(type_total, dtype=jnp.int32)
    kind_onehot = (atom_types[:, None] == type_ids[None, :]).astype(jnp.float32)
    atom_mass = jnp.dot(kind_onehot, masses, precision=highest)
    momenta_half, thermo_half = chain_half(momenta, thermostat, atom_mass)
    velocity = momenta_half / atom_mass
    matrix = cycle_matrices(NBEADS)
    stacked = jnp.stack([positions, velocity], axis=1)
    mixed = jnp.einsum(
        "xyjn,nycs->jxcs",
        matrix,
        lax.all_to_all(stacked, "bead", split_axis=3, concat_axis=0, tiled=True),
        precision=highest,
    )
    moved_pair = lax.all_to_all(mixed, "bead", split_axis=0, concat_axis=3, tiled=True)
    drifted = moved_pair[:, 0]
    momenta_drift = moved_pair[:, 1] * atom_mass
    payload = jnp.concatenate(
        [drifted, momenta_drift, thermo_half.reshape(bead_local, 3 * CHAIN, slot_total)], axis=1
    )
    row_lists = move_rows[0]
    live_counts = move_count[0]
    slot_order = jnp.arange(row_lists.shape[1], dtype=jnp.int32)

    def outgoing(class_index):
        leaving = jnp.take(payload, row_lists[class_index], axis=2)
        leaving = leaving.at[:, 0].add(-offsets[class_index] * slab_width)
        return (leaving, jnp.take(atom_types, row_lists[class_index]))

    arrivals = [outgoing(0), outgoing(1), outgoing(2), outgoing(3)]
    for class_index in range(4):
        arrivals[class_index] = shifted(arrivals[class_index], "space", offsets[class_index])
    landing = []
    for class_index in range(4):
        partner = opposite[class_index]
        landing.append(jnp.where(slot_order < live_counts[partner], row_lists[partner], slot_total))
    landing = jnp.concatenate(landing)
    arrived = jnp.concatenate([arrivals[class_index][0] for class_index in range(4)], axis=2)
    arrived_kinds = jnp.concatenate([arrivals[class_index][1] for class_index in range(4)])
    migrated = payload.at[:, :, landing].set(arrived, mode="drop")
    new_types = atom_types.at[landing].set(arrived_kinds, mode="drop")
    cell_total = slot_total // CAP
    new_positions = migrated[:, :3]
    cell_grid = new_positions.reshape(bead_local, 3, cell_total, CAP)
    type_grid = new_types.reshape(1, 1, cell_total, CAP)
    extended, wide_types = (
        extended_2(cell_grid, (("space", 2),), cell_total),
        extended_2(type_grid, (("space", 2),), cell_total),
    )
    frame_shift = jnp.repeat(
        jnp.array([-slab_width, 0.0, slab_width], dtype=jnp.float32), cell_total
    )
    extended = extended.at[:, 0].add(frame_shift[:, None])
    flat_types = wide_types.reshape(3 * cell_total, CAP)
    own_onehot = (new_types[:, None] == type_ids[None, :]).astype(jnp.bfloat16)
    own_table = jnp.dot(own_onehot, pair_table, preferred_element_type=jnp.float32).astype(
        jnp.bfloat16
    )
    own_table = own_table.reshape(cell_total, CAP, type_total)
    inverse_width = 0.5 / (pair_reach * pair_reach)
    pair_scale = 1.0 / (pair_reach * pair_reach * NBEADS)
    tile_lists = tile_pairs[0]
    live_tiles = tile_count[0]

    def block_step(block_index, running):
        first_tile = block_index * tile_block
        cells_near = lax.dynamic_slice_in_dim(tile_lists[0], first_tile, tile_block)
        cells_far = lax.dynamic_slice_in_dim(tile_lists[1], first_tile, tile_block)
        live_mask = (first_tile + jnp.arange(tile_block, dtype=jnp.int32) < live_tiles).astype(
            jnp.float32
        )
        near_cells = jnp.take(cell_grid, cells_near, axis=2)
        far_cells = jnp.take(extended, cells_far, axis=2)
        far_onehot = (jnp.take(flat_types, cells_far, axis=0)[:, :, None] == type_ids).astype(
            jnp.bfloat16
        )
        strength = jnp.einsum(
            "tan,tbn->tab",
            jnp.take(own_table, cells_near, axis=0),
            far_onehot,
            preferred_element_type=jnp.float32,
        )
        strength = strength * live_mask[:, None, None]
        delta_x = near_cells[:, 0, :, :, None] - far_cells[:, 0, :, None, :]
        delta_y = near_cells[:, 1, :, :, None] - far_cells[:, 1, :, None, :]
        delta_z = near_cells[:, 2, :, :, None] - far_cells[:, 2, :, None, :]
        distance = delta_x * delta_x + delta_y * delta_y + delta_z * delta_z
        weight = strength * jnp.exp(-distance * inverse_width) * pair_scale
        pair_force = jnp.stack(
            [
                jnp.sum(weight * delta_x, axis=3),
                jnp.sum(weight * delta_y, axis=3),
                jnp.sum(weight * delta_z, axis=3),
            ],
            axis=1,
        )
        return running.at[:, :, cells_near].add(pair_force)

    block_count = tile_lists.shape[1] // tile_block
    forces = lax.fori_loop(0, block_count, block_step, jnp.zeros_like(cell_grid)).reshape(
        bead_local, 3, slot_total
    )
    momenta_out = migrated[:, 3:6] + inner_step * forces
    thermo_out = migrated[:, 6:].reshape(bead_local, CHAIN, 3, slot_total)
    return (new_positions, momenta_out, thermo_out, forces, new_types)


def solution(mesh):
    placed = (
        P("bead", None, "space"),
        P("bead", None, "space"),
        P("bead", None, None, "space"),
        P("space"),
        P(),
        P(),
        P("space", None, None),
        P("space"),
        P("space", None, None),
        P("space", None),
    )
    return jax.shard_map(
        per_device,
        mesh=mesh,
        in_specs=placed,
        out_specs=(
            P("bead", None, "space"),
            P("bead", None, "space"),
            P("bead", None, None, "space"),
            P("bead", None, "space"),
            P("space"),
        ),
        check_vma=False,
    )
```

profile of v0, /device:TPU:31, one launch (start us, length us, event | category | flops | bytes accessed | tf_op | source)
XLA Modules:
  0.0 779.5 jit_solution(954869878154648173)
XLA Ops:
  3.8 4.6 fusion.21
  11.2 11.8 %copy.211 = f32[2,2,3,6144]{2,0,1,3:T(2,128)} copy(f32[2,2,3,6144]{3,0,2,1:T(2,128)S(1)} %pad_maximum_fusion.3) | data formatting | bytes 589824 | tf_op jit(solution)/shard_map/stack | solution.py:116
  23.0 21.4 %reshape.690 = f32[8,1,9216]{2,1,0:T(1,128)} reshape(f32[6144,2,2,3]{3,2,1,0:T(2,128)} %bitcast.192) | data formatting | bytes 589824
  44.4 8.2 %all-to-all-start = ((f32[8,1,9216]{2,1,0:T(1,128)}), f32[8,1,9216]{2,1,0:T(1,128)S(1)}, u32[]{:S(2)}, u32[]{:S(2)}) async-start(f32[8,1,9216]{2,1,0:T(1,128)} %reshape.690), calls=%async_computation | async-start | bytes 589824 | tf_op jit(solution)/shard_map/all_to_all | solution.py:120
  55.5 4.4 collective-permute-start.6
  63.8 3.8 collective-permute-start.4
  71.1 23.7 %reshape.691 = f32[6144,2,2,3]{3,2,1,0:T(2,128)} reshape(f32[8,9216]{1,0:T(8,128)S(1)} %reduce.12) | data formatting | bytes 589824
  94.8 15.4 %copy.212 = f32[2,2,3,8,768]{4,0,3,1,2:T(2,128)S(1)} copy(f32[2,2,3,8,768]{2,0,1,4,3:T(2,128)} %bitcast.193) | data formatting | bytes 589824 | tf_op jit(solution)/shard_map/all_to_all | solution.py:120
  111.9 6.6 all-to-all-start.1
  118.8 5.9 copy.217
  129.7 5.9 copy.216
  135.6 5.9 copy.215
  141.5 16.3 %pad_maximum_fusion = f32[2,18,6144]{1,0,2:T(2,128)} fusion(f32[2,12,6144]{1,0,2:T(2,128)} %copy.217, f32[2,3,6144]{1,0,2:T(2,128)} %copy.216, f32[2,3,6144]{1,0,2:T(2,128)} %copy.215), kind=kLoop, calls=%fused_computation.64 | loop fusion | flops 442368 | bytes 1769472 | tf_op jit(solution)/shard_map/concatenate | solution.py:126
  161.3 3.5 gather_fusion.6
  164.8 3.5 gather_fusion.5
  168.2 3.5 gather_fusion.4
  183.6 4.8 collective-permute-start.2
  188.5 5.1 collective-permute-start
  196.7 5.2 collective-permute-start.8
  202.7 35.2 %scatter_fusion.1 = f32[2,18,6144]{1,0,2:T(2,128)} fusion(f32[2,18,6144]{1,0,2:T(2,128)} %pad_maximum_fusion, s32[384]{0:T(512)S(1)} %fusion.59, f32[384,2,18]{2,1,0:T(2,128)S(1)} %copy.222), kind=kCustom, calls=%fused_computation.13 | custom fusion | bytes 167424 | tf_op jit(solution)/shard_map/scatter | solution.py:148
  237.9 13.9 %fusion.74 = (f32[2,3,6144]{1,0,2:T(2,128)}, f32[2,3,6144]{1,0,2:T(2,128)}) fusion(f32[2,18,6144]{1,0,2:T(2,128)} %scatter_fusion.1), kind=kLoop, calls=%fused_computation.188 | loop fusion | bytes 589824 | tf_op jit(solution)/shard_map/slice | solution.py:211
  251.8 7.9 %copy.227 = f32[2,3,48,128]{3,0,2,1:T(2,128)} copy(f32[2,3,48,128]{1,0,3,2:T(2,128)} %bitcast.191) | data formatting | bytes 294912
  259.7 5.1 collective-permute-start.10
  268.2 7.9 %copy.229 = f32[2,3,6144]{2,0,1:T(2,128)} copy(f32[2,3,6144]{1,0,2:T(2,128)} %get-tuple-element.365) | data formatting | bytes 294912
  276.1 10.2 %slice.307 = f32[2,12,6144]{1,0,2:T(2,128)} slice(f32[2,18,6144]{1,0,2:T(2,128)} %scatter_fusion.1), slice={[0:2], [6:18], [0:6144]} | slice | bytes 1179648 | tf_op jit(solution)/shard_map/slice | solution.py:212
  286.3 7.9 %copy.237 = f32[2,3,6144]{2,0,1:T(2,128)} copy(f32[2,3,6144]{1,0,2:T(2,128)} %get-tuple-element.364) | data formatting | bytes 294912
  294.2 7.1 copy.228
  306.8 470.8 %while.19 = (s32[]{:T(128)}, f32[2,3,48,128]{3,0,2,1:T(2,128)}, s32[2,672]{1,0:T(2,128)S(1)}, bf16[48,128,128]{2,1,0:T(8,128)(2,1)S(1)}, s32[144,128]{1,0:T(8,12...) while((s32[]{:T(128)}, f32[2,3,48,128]{3,0,2,1:T(2,128)}, ...), condition=%wide.region_10.13_spmd.clone, body=%wide.region_5.0_spmd.clone.sunk | while | flops 270846112 | bytes 17484328 | solution.py:208
  317.5 5.8 fusion.86
  323.3 15.1 %fusion.87 = (f32[2,56,128]{2,1,0:T(8,128)S(1)}, f32[2,56,128]{2,1,0:T(8,128)S(1)}, f32[2,56,128]{2,1,0:T(8,128)S(1)}) fusion(f32[2,56,128]{2,1,0:T(8,128)S(1)} %copy.268, f32[2,56,128]{2,1,0:T(8,128)} %copy.269, f32[2,56,128]{2,1,0:T(8,128)} %copy.270, f32[2,56,128]{2,1,0:T(8,128)} %copy.271, f32[2,56,128]{2,1,0:T(8,128)} %copy.272, ...), kind=kLoop, calls=%fused_computation.29.clone.1 | loop fusion | flops 32987136 | bytes 4186112 | tf_op jit(solution)/shard_map/while/body/eval_jaxpr/reduce_sum | solution.py:199
  338.5 7.5 scatter_fusion
  356.7 5.8 fusion.86
  362.6 15.1 %fusion.87 = (f32[2,56,128]{2,1,0:T(8,128)S(1)}, f32[2,56,128]{2,1,0:T(8,128)S(1)}, f32[2,56,128]{2,1,0:T(8,128)S(1)}) fusion(f32[2,56,128]{2,1,0:T(8,128)S(1)} %copy.268, f32[2,56,128]{2,1,0:T(8,128)} %copy.269, f32[2,56,128]{2,1,0:T(8,128)} %copy.270, f32[2,56,128]{2,1,0:T(8,128)} %copy.271, f32[2,56,128]{2,1,0:T(8,128)} %copy.272, ...), kind=kLoop, calls=%fused_computation.29.clone.1 | loop fusion | flops 32987136 | bytes 4186112 | tf_op jit(solution)/shard_map/while/body/eval_jaxpr/reduce_sum | solution.py:199
  377.8 7.5 scatter_fusion
  395.9 5.8 fusion.86
  401.8 15.1 %fusion.87 = (f32[2,56,128]{2,1,0:T(8,128)S(1)}, f32[2,56,128]{2,1,0:T(8,128)S(1)}, f32[2,56,128]{2,1,0:T(8,128)S(1)}) fusion(f32[2,56,128]{2,1,0:T(8,128)S(1)} %copy.268, f32[2,56,128]{2,1,0:T(8,128)} %copy.269, f32[2,56,128]{2,1,0:T(8,128)} %copy.270, f32[2,56,128]{2,1,0:T(8,128)} %copy.271, f32[2,56,128]{2,1,0:T(8,128)} %copy.272, ...), kind=kLoop, calls=%fused_computation.29.clone.1 | loop fusion | flops 32987136 | bytes 4186112 | tf_op jit(solution)/shard_map/while/body/eval_jaxpr/reduce_sum | solution.py:199
  417.0 7.5 scatter_fusion
  435.1 5.8 fusion.86
  441.0 15.1 %fusion.87 = (f32[2,56,128]{2,1,0:T(8,128)S(1)}, f32[2,56,128]{2,1,0:T(8,128)S(1)}, f32[2,56,128]{2,1,0:T(8,128)S(1)}) fusion(f32[2,56,128]{2,1,0:T(8,128)S(1)} %copy.268, f32[2,56,128]{2,1,0:T(8,128)} %copy.269, f32[2,56,128]{2,1,0:T(8,128)} %copy.270, f32[2,56,128]{2,1,0:T(8,128)} %copy.271, f32[2,56,128]{2,1,0:T(8,128)} %copy.272, ...), kind=kLoop, calls=%fused_computation.29.clone.1 | loop fusion | flops 32987136 | bytes 4186112 | tf_op jit(solution)/shard_map/while/body/eval_jaxpr/reduce_sum | solution.py:199
  456.2 7.5 scatter_fusion
  474.4 5.8 fusion.86
  480.2 15.1 %fusion.87 = (f32[2,56,128]{2,1,0:T(8,128)S(1)}, f32[2,56,128]{2,1,0:T(8,128)S(1)}, f32[2,56,128]{2,1,0:T(8,128)S(1)}) fusion(f32[2,56,128]{2,1,0:T(8,128)S(1)} %copy.268, f32[2,56,128]{2,1,0:T(8,128)} %copy.269, f32[2,56,128]{2,1,0:T(8,128)} %copy.270, f32[2,56,128]{2,1,0:T(8,128)} %copy.271, f32[2,56,128]{2,1,0:T(8,128)} %copy.272, ...), kind=kLoop, calls=%fused_computation.29.clone.1 | loop fusion | flops 32987136 | bytes 4186112 | tf_op jit(solution)/shard_map/while/body/eval_jaxpr/reduce_sum | solution.py:199
  495.4 7.5 scatter_fusion
  513.6 5.8 fusion.86
  519.4 15.1 %fusion.87 = (f32[2,56,128]{2,1,0:T(8,128)S(1)}, f32[2,56,128]{2,1,0:T(8,128)S(1)}, f32[2,56,128]{2,1,0:T(8,128)S(1)}) fusion(f32[2,56,128]{2,1,0:T(8,128)S(1)} %copy.268, f32[2,56,128]{2,1,0:T(8,128)} %copy.269, f32[2,56,128]{2,1,0:T(8,128)} %copy.270, f32[2,56,128]{2,1,0:T(8,128)} %copy.271, f32[2,56,128]{2,1,0:T(8,128)} %copy.272, ...), kind=kLoop, calls=%fused_computation.29.clone.1 | loop fusion | flops 32987136 | bytes 4186112 | tf_op jit(solution)/shard_map/while/body/eval_jaxpr/reduce_sum | solution.py:199
  534.6 7.5 scatter_fusion
  552.8 5.8 fusion.86
  558.7 15.1 %fusion.87 = (f32[2,56,128]{2,1,0:T(8,128)S(1)}, f32[2,56,128]{2,1,0:T(8,128)S(1)}, f32[2,56,128]{2,1,0:T(8,128)S(1)}) fusion(f32[2,56,128]{2,1,0:T(8,128)S(1)} %copy.268, f32[2,56,128]{2,1,0:T(8,128)} %copy.269, f32[2,56,128]{2,1,0:T(8,128)} %copy.270, f32[2,56,128]{2,1,0:T(8,128)} %copy.271, f32[2,56,128]{2,1,0:T(8,128)} %copy.272, ...), kind=kLoop, calls=%fused_computation.29.clone.1 | loop fusion | flops 32987136 | bytes 4186112 | tf_op jit(solution)/shard_map/while/body/eval_jaxpr/reduce_sum | solution.py:199
  573.9 7.5 scatter_fusion
  592.0 5.8 fusion.86
  597.9 15.1 %fusion.87 = (f32[2,56,128]{2,1,0:T(8,128)S(1)}, f32[2,56,128]{2,1,0:T(8,128)S(1)}, f32[2,56,128]{2,1,0:T(8,128)S(1)}) fusion(f32[2,56,128]{2,1,0:T(8,128)S(1)} %copy.268, f32[2,56,128]{2,1,0:T(8,128)} %copy.269, f32[2,56,128]{2,1,0:T(8,128)} %copy.270, f32[2,56,128]{2,1,0:T(8,128)} %copy.271, f32[2,56,128]{2,1,0:T(8,128)} %copy.272, ...), kind=kLoop, calls=%fused_computation.29.clone.1 | loop fusion | flops 32987136 | bytes 4186112 | tf_op jit(solution)/shard_map/while/body/eval_jaxpr/reduce_sum | solution.py:199
  613.1 7.5 scatter_fusion
  631.2 5.8 fusion.86
  637.1 15.1 %fusion.87 = (f32[2,56,128]{2,1,0:T(8,128)S(1)}, f32[2,56,128]{2,1,0:T(8,128)S(1)}, f32[2,56,128]{2,1,0:T(8,128)S(1)}) fusion(f32[2,56,128]{2,1,0:T(8,128)S(1)} %copy.268, f32[2,56,128]{2,1,0:T(8,128)} %copy.269, f32[2,56,128]{2,1,0:T(8,128)} %copy.270, f32[2,56,128]{2,1,0:T(8,128)} %copy.271, f32[2,56,128]{2,1,0:T(8,128)} %copy.272, ...), kind=kLoop, calls=%fused_computation.29.clone.1 | loop fusion | flops 32987136 | bytes 4186112 | tf_op jit(solution)/shard_map/while/body/eval_jaxpr/reduce_sum | solution.py:199
  652.3 7.5 scatter_fusion
  670.5 5.8 fusion.86
  676.3 15.1 %fusion.87 = (f32[2,56,128]{2,1,0:T(8,128)S(1)}, f32[2,56,128]{2,1,0:T(8,128)S(1)}, f32[2,56,128]{2,1,0:T(8,128)S(1)}) fusion(f32[2,56,128]{2,1,0:T(8,128)S(1)} %copy.268, f32[2,56,128]{2,1,0:T(8,128)} %copy.269, f32[2,56,128]{2,1,0:T(8,128)} %copy.270, f32[2,56,128]{2,1,0:T(8,128)} %copy.271, f32[2,56,128]{2,1,0:T(8,128)} %copy.272, ...), kind=kLoop, calls=%fused_computation.29.clone.1 | loop fusion | flops 32987136 | bytes 4186112 | tf_op jit(solution)/shard_map/while/body/eval_jaxpr/reduce_sum | solution.py:199
  691.5 7.5 scatter_fusion
  709.7 5.8 fusion.86
  715.5 15.1 %fusion.87 = (f32[2,56,128]{2,1,0:T(8,128)S(1)}, f32[2,56,128]{2,1,0:T(8,128)S(1)}, f32[2,56,128]{2,1,0:T(8,128)S(1)}) fusion(f32[2,56,128]{2,1,0:T(8,128)S(1)} %copy.268, f32[2,56,128]{2,1,0:T(8,128)} %copy.269, f32[2,56,128]{2,1,0:T(8,128)} %copy.270, f32[2,56,128]{2,1,0:T(8,128)} %copy.271, f32[2,56,128]{2,1,0:T(8,128)} %copy.272, ...), kind=kLoop, calls=%fused_computation.29.clone.1 | loop fusion | flops 32987136 | bytes 4186112 | tf_op jit(solution)/shard_map/while/body/eval_jaxpr/reduce_sum | solution.py:199
  730.7 7.5 scatter_fusion
  748.9 5.8 fusion.86
  754.7 15.1 %fusion.87 = (f32[2,56,128]{2,1,0:T(8,128)S(1)}, f32[2,56,128]{2,1,0:T(8,128)S(1)}, f32[2,56,128]{2,1,0:T(8,128)S(1)}) fusion(f32[2,56,128]{2,1,0:T(8,128)S(1)} %copy.268, f32[2,56,128]{2,1,0:T(8,128)} %copy.269, f32[2,56,128]{2,1,0:T(8,128)} %copy.270, f32[2,56,128]{2,1,0:T(8,128)} %copy.271, f32[2,56,128]{2,1,0:T(8,128)} %copy.272, ...), kind=kLoop, calls=%fused_computation.29.clone.1 | loop fusion | flops 32987136 | bytes 4186112 | tf_op jit(solution)/shard_map/while/body/eval_jaxpr/reduce_sum | solution.py:199
  769.9 7.6 scatter_fusion
  (403 shorter events, 181.5 us)
Async XLA Ops:
  0.6 264.1 %copy-start = (bf16[128,128]{1,0:T(8,128)(2,1)S(1)}, bf16[128,128]{1,0:T(8,128)(2,1)}, u32[]{:S(2)}) copy-start(bf16[128,128]{1,0:T(8,128)(2,1)} %param.32) | copy-start | bytes 98308
  23.0 29.6 %copy-start.5 = (s32[1,4,96]{2,1,0:T(4,128)S(1)}, s32[1,4,96]{2,1,0:T(4,128)}, u32[]{:S(2)}) copy-start(s32[1,4,96]{2,1,0:T(4,128)} %param.35) | copy-start | bytes 4612
  44.4 24.8 %all-to-all-start = ((f32[8,1,9216]{2,1,0:T(1,128)}), f32[8,1,9216]{2,1,0:T(1,128)S(1)}, u32[]{:S(2)}, u32[]{:S(2)}) async-start(f32[8,1,9216]{2,1,0:T(1,128)} %reshape.690), calls=%async_computation | async-start | bytes 589824 | tf_op jit(solution)/shard_map/all_to_all | solution.py:120
  53.8 129.8 %collective-permute-start.7 = (s32[96]{0:T(128)S(1)}, s32[96]{0:T(128)S(1)}, u32[]{:S(2)}, u32[]{:S(2)}) collective-permute-start(s32[96]{0:T(128)S(1)} %broadcast_select_fusion.1), channel_id=1, source_target_pairs={{0,30},{1,31},{2,0},{3,1},{4,2},{5,3},{6,4},{7,5},{8,6},{9,7},{10,... | collective-permute-start | bytes 1160 | tf_op jit(solution)/shard_map/ppermute | solution.py:28
  55.5 133.0 %collective-permute-start.6 = (s32[96]{0:T(128)S(1)}, s32[96]{0:T(128)S(1)}, u32[]{:S(2)}, u32[]{:S(2)}) collective-permute-start(s32[96]{0:T(128)S(1)} %broadcast_select_fusion.2), channel_id=1, source_target_pairs={{0,2},{1,3},{2,4},{3,5},{4,6},{5,7},{6,8},{7,9},{8,10},{9,11},{10,... | collective-permute-start | bytes 1160 | tf_op jit(solution)/shard_map/ppermute | solution.py:28
  61.1 127.4 %collective-permute-start.5 = (s32[96]{0:T(128)S(1)}, s32[96]{0:T(128)S(1)}, u32[]{:S(2)}, u32[]{:S(2)}) collective-permute-start(s32[96]{0:T(128)S(1)} %broadcast_select_fusion.3), channel_id=1, source_target_pairs={{0,31},{1,0},{2,1},{3,2},{4,3},{5,4},{6,5},{7,6},{8,7},{9,8},{10,9... | collective-permute-start | bytes 1160 | tf_op jit(solution)/shard_map/ppermute | solution.py:28
  63.8 129.7 %collective-permute-start.4 = (s32[96]{0:T(128)S(1)}, s32[96]{0:T(128)S(1)}, u32[]{:S(2)}, u32[]{:S(2)}) collective-permute-start(s32[96]{0:T(128)S(1)} %broadcast_select_fusion.4), channel_id=1, source_target_pairs={{0,1},{1,2},{2,3},{3,4},{4,5},{5,6},{6,7},{7,8},{8,9},{9,10},{10,1... | collective-permute-start | bytes 1160 | tf_op jit(solution)/shard_map/ppermute | solution.py:28
  110.3 14.5 %copy-start.7 = (f32[3]{0:T(128)S(1)}, f32[3]{0:T(128)}, u32[]{:S(2)}) copy-start(f32[3]{0:T(128)} %constant.355.clone) | copy-start | bytes 40
  110.3 14.6 %copy-start.6 = (s32[1,4]{1,0:T(1,128)S(1)}, s32[1,4]{1,0:T(1,128)}, u32[]{:S(2)}) copy-start(s32[1,4]{1,0:T(1,128)} %param.36) | copy-start | bytes 52
  111.9 17.5 %all-to-all-start.1 = ((f32[16,2,3,768]{3,1,2,0:T(2,128)}), f32[16,2,3,768]{3,1,2,0:T(2,128)S(1)}, u32[]{:S(2)}, u32[]{:S(2)}) async-start(f32[16,2,3,768]{3,1,2,0:T(2,128)} %copy.213), calls=%async_computation.1 | async-start | bytes 589824 | tf_op jit(solution)/shard_map/all_to_all | solution.py:123
  174.6 22.1 %collective-permute-start.3 = (f32[2,18,96]{1,0,2:T(2,128)S(1)}, f32[2,18,96]{1,0,2:T(2,128)S(1)}, u32[]{:S(2)}, u32[]{:S(2)}) collective-permute-start(f32[2,18,96]{1,0,2:T(2,128)S(1)} %scatter-add.39), channel_id=1, source_target_pairs={{0,30},{1,31},{2,0},{3,1},{4,2},{5,3},{6,4},{7,5},{8,6},{9,7},{10,... | collective-permute-start | bytes 41480 | tf_op jit(solution)/shard_map/ppermute | solution.py:28
  183.6 18.4 %collective-permute-start.2 = (f32[2,18,96]{1,0,2:T(2,128)S(1)}, f32[2,18,96]{1,0,2:T(2,128)S(1)}, u32[]{:S(2)}, u32[]{:S(2)}) collective-permute-start(f32[2,18,96]{1,0,2:T(2,128)S(1)} %scatter-add.38), channel_id=1, source_target_pairs={{0,2},{1,3},{2,4},{3,5},{4,6},{5,7},{6,8},{7,9},{8,10},{9,11},{10,... | collective-permute-start | bytes 41480 | tf_op jit(solution)/shard_map/ppermute | solution.py:28
  188.5 13.6 %collective-permute-start.1 = (f32[2,18,96]{1,0,2:T(2,128)S(1)}, f32[2,18,96]{1,0,2:T(2,128)S(1)}, u32[]{:S(2)}, u32[]{:S(2)}) collective-permute-start(f32[2,18,96]{1,0,2:T(2,128)S(1)} %scatter-add.37), channel_id=1, source_target_pairs={{0,31},{1,0},{2,1},{3,2},{4,3},{5,4},{6,5},{7,6},{8,7},{9,8},{10,9... | collective-permute-start | bytes 41480 | tf_op jit(solution)/shard_map/ppermute | solution.py:28
  188.5 13.7 %collective-permute-start = (f32[2,18,96]{1,0,2:T(2,128)S(1)}, f32[2,18,96]{1,0,2:T(2,128)S(1)}, u32[]{:S(2)}, u32[]{:S(2)}) collective-permute-start(f32[2,18,96]{1,0,2:T(2,128)S(1)} %scatter-add.36), channel_id=1, source_target_pairs={{0,1},{1,2},{2,3},{3,4},{4,5},{5,6},{6,7},{7,8},{8,9},{9,10},{10,1... | collective-permute-start | bytes 41480 | tf_op jit(solution)/shard_map/ppermute | solution.py:28
  196.6 71.5 %copy-start.2 = (s32[6144]{0:T(1024)}, s32[6144]{0:T(1024)S(1)}, u32[]{:S(2)}) copy-start(s32[6144]{0:T(1024)S(1)} %scatter_fusion.2) | copy-start | bytes 73732
  196.6 71.5 %collective-permute-start.9 = (s32[1,1,48,128]{3,2,1,0:T(8,128)S(1)}, s32[1,1,48,128]{3,2,1,0:T(8,128)S(1)}, u32[]{:S(2)}, u32[]{:S(2)}) collective-permute-start(s32[1,1,48,128]{3,2,1,0:T(8,128)S(1)} %bitcast.187), channel_id=1, source_target_pairs={{1,0},{2,1},{3,2},{4,3},{5,4},{6,5},{7,6},{8,7},{9,8},{10,9},{11,1... | collective-permute-start | bytes 73736 | tf_op jit(solution)/shard_map/ppermute | solution.py:39
  196.7 71.4 %collective-permute-start.8 = (s32[1,1,48,128]{3,2,1,0:T(8,128)S(1)}, s32[1,1,48,128]{3,2,1,0:T(8,128)S(1)}, u32[]{:S(2)}, u32[]{:S(2)}) collective-permute-start(s32[1,1,48,128]{3,2,1,0:T(8,128)S(1)} %bitcast.188), channel_id=1, source_target_pairs={{0,1},{1,2},{2,3},{3,4},{4,5},{5,6},{6,7},{7,8},{8,9},{9,10},{10,1... | collective-permute-start | bytes 73736 | tf_op jit(solution)/shard_map/ppermute | solution.py:38
  259.7 42.7 %collective-permute-start.11 = (f32[2,3,48,128]{3,0,2,1:T(2,128)}, f32[2,3,48,128]{3,0,2,1:T(2,128)S(1)}, u32[]{:S(2)}, u32[]{:S(2)}) collective-permute-start(f32[2,3,48,128]{3,0,2,1:T(2,128)} %copy.227), channel_id=1, source_target_pairs={{1,0},{2,1},{3,2},{4,3},{5,4},{6,5},{7,6},{8,7},{9,8},{10,9},{11,1... | collective-permute-start | bytes 442376 | tf_op jit(solution)/shard_map/ppermute | solution.py:39
  259.7 42.7 %collective-permute-start.10 = (f32[2,3,48,128]{3,0,2,1:T(2,128)}, f32[2,3,48,128]{3,0,2,1:T(2,128)S(1)}, u32[]{:S(2)}, u32[]{:S(2)}) collective-permute-start(f32[2,3,48,128]{3,0,2,1:T(2,128)} %copy.227), channel_id=1, source_target_pairs={{0,1},{1,2},{2,3},{3,4},{4,5},{5,6},{6,7},{7,8},{8,9},{9,10},{10,1... | collective-permute-start | bytes 442376 | tf_op jit(solution)/shard_map/ppermute | solution.py:38
  294.2 12.6 %copy-start.3 = (s32[1,2,672]{2,1,0:T(2,128)S(1)}, s32[1,2,672]{2,1,0:T(2,128)}, u32[]{:S(2)}) copy-start(s32[1,2,672]{2,1,0:T(2,128)} %param.33) | copy-start | bytes 16132
  308.8 2.0 copy-start.4
  348.0 2.0 copy-start.4
  387.2 2.0 copy-start.4
  426.4 2.0 copy-start.4
  465.7 2.0 copy-start.4
  504.9 2.0 copy-start.4
  544.1 2.0 copy-start.4
  583.3 2.0 copy-start.4
  622.5 2.0 copy-start.4
  661.8 2.0 copy-start.4
  701.0 2.0 copy-start.4
  740.2 2.0 copy-start.4
  777.5 1.8 copy-start.1
where the time goes:
time: 793 us; the launch traced here: 779 us
  other arithmetic  331 us (42%)
  local copies, waits for them, and re-layouts  320 us (40%)
  matrix products  78.5 us (10%)
  starting transfers between devices  45.9 us (6%)
    reduce_sum x12, other arithmetic, block_step(): jnp.sum(weight * delta_x, axis=3)  181 us
    scatter-add x12, other arithmetic, block_step(): return running.at[:, :, cells_near].add(pair_force)  89.8 us
    unnamed x21, local copies, waits for them, and re-layouts  70.8 us
    dot_general x12, matrix products, block_step(): jnp.einsum('tan,tbn->tab', jnp.take(own_table, cells_near, axis=0), far_o...  70.1 us
    scatter x1, local copies, waits for them, and re-layouts, per_device(): migrated = payload.at[:, :, landing].set(arrived, mode='drop')  35.2 us
    gather x12, local copies, waits for them, and re-layouts, block_step(): far_cells = jnp.take(extended, cells_far, axis=2)  21.7 us
    ppermute x8, starting transfers between devices, shifted(): lax.ppermute(shard, axis, [(i, (i + by) % count) for i in range(count)])  20.7 us
    gather x12, local copies, waits for them, and re-layouts, block_step(): near_cells = jnp.take(cell_grid, cells_near, axis=2)  20.5 us
  transfers between devices with their start and end apart: 14, of which 1 were waited for; matrix products, arithmetic and copies ran while one was open for 27% of the time, Pallas kernels for 0%

commit v1 on v0

v1 whole, which is shorter than its diff:
```python
import functools
import math

import jax
import jax.numpy as jnp
import numpy as np
from jax import lax
from jax.experimental import pallas as pl
from jax.experimental.pallas import tpu as pltpu
from jax.sharding import PartitionSpec as P

NBEADS = 16
CAP = 128
CHAIN = 4
NTYPES = 128
outer_step = 0.2
inner_step = 0.05
thermal = 1.0
chain_mass = 2.0
cycle_freq = 2.0
pair_reach = 0.4
offsets = (1, -1, 2, -2)
opposite = (1, 0, 3, 2)
MESH = pl.DeviceIdType.MESH
f32 = jnp.float32
bf16 = jnp.bfloat16

reach2 = pair_reach * pair_reach
spread = math.sqrt(1.0 / (reach2 * math.log(2.0)))
log_scale = math.log2(1.0 / (reach2 * NBEADS))
centre = (0.5, 4.0, 3.0)
batch = 8
prep_unroll = 8
halo_parts = 4


def split3(x):
    a = x.astype(bf16).astype(f32)
    b = (x - a).astype(bf16).astype(f32)
    return a, b, x - a - b


def cycle_map(peers):
    k = np.arange(NBEADS)
    w = 2.0 * cycle_freq * np.sin(math.pi * k / NBEADS)
    r = outer_step * w
    c = np.cos(r)
    s = np.where(k > 0, np.sin(r) / np.where(k > 0, w, 1.0), outer_step)
    b = -w * np.sin(r)
    lag = (k[:, None] - k[None, :]) % NBEADS
    phase = np.cos(2.0 * math.pi / NBEADS * (lag[:, :, None] * k % NBEADS))
    mc, ms, mb = ((phase * v).sum(2) / NBEADS for v in (c, s, b))
    maps = [[mc, ms], [mb, mc]]
    per = NBEADS // peers
    size = peers * 8
    big = np.zeros((3 * size, 3 * size))

    def place(p, kind, bead, comp, half):
        row = (kind * per + bead) * 3 + comp
        if row < 8:
            return half * size + p * 8 + row
        return 2 * size + p * 8 + half * 4 + row - 8

    for half in range(2):
        for comp in range(3):
            for kind in range(2):
                for kind2 in range(2):
                    for j in range(NBEADS):
                        for i in range(NBEADS):
                            to = place(j // per, kind, j % per, comp, half)
                            fro = place(i // per, kind2, i % per, comp, half)
                            big[to, fro] = maps[kind][kind2][j, i]
    return big.astype(np.float32)


def front_kernel(
    peers, domains,
    pos, mom, thermo, types, masses, rows, count, bigm,
    ext, momo, tho,
    send1, recv1, send2, recv2, pd, pth, mass, mask, inverse, into, gat, sca,
    e_out, e_in, l_out, l_in,
    s1, r1, s2, r2, se, re, sl, rl, sh, rh,
):
    slots = pos.shape[2]
    chunk = slots // peers
    half = chunk // 2
    me_b = lax.axis_index("bead")
    me_s = lax.axis_index("space")

    def ring(off):
        return lax.rem(me_b + off + peers, peers)

    def domain(off):
        return lax.rem(me_s + off + domains, domains)

    def lanes(start, size, unit=128):
        return pl.ds(pl.multiple_of(start, unit), size)

    barrier = pltpu.get_barrier_semaphore()
    for off in range(1, peers):
        pl.semaphore_signal(barrier, inc=1, device_id=(ring(off), me_s), device_id_type=MESH)
    for off in offsets:
        pl.semaphore_signal(barrier, inc=1, device_id=(me_b, domain(off)), device_id_type=MESH)

    m1, m2, m3 = split3(masses[...])
    mass_rows = jnp.concatenate([m1, m2, m3, jnp.zeros((5, NTYPES), f32)], axis=0).astype(bf16)
    kind_iota = lax.broadcasted_iota(jnp.int32, (NTYPES, chunk), 0)

    def find_mass(n, carry):
        at = lanes(n * chunk, chunk)
        kind = jnp.broadcast_to(types[:, at], (NTYPES, chunk))
        onehot = jnp.where(kind == kind_iota, 1.0, 0.0).astype(bf16)
        got = jnp.dot(mass_rows, onehot, preferred_element_type=f32)
        found = got[0:1] + got[1:2] + got[2:3]
        mass[:, at] = found
        inverse[:, at] = 1.0 / found
        return carry

    lax.fori_loop(0, peers, find_mass, 0)
    pl.semaphore_wait(barrier, peers - 1 + len(offsets))

    def chain(p):
        at = lanes(p * chunk, chunk)
        inv = inverse[:, at]
        h = 0.5 * outer_step
        vel = []
        for bead in range(2):
            z = [thermo[bead, link, :, at] for link in range(CHAIN)]
            q = mom[bead, :, at]
            old = [q * q * inv * (1.0 / chain_mass)] + [v * v for v in z[:-1]]
            z[3] = z[3] + h * (old[3] - thermal / chain_mass)
            for link in (2, 1, 0):
                drive = old[link] - thermal / chain_mass
                z[link] = z[link] * jnp.exp(z[link + 1] * -h) + h * drive
            for link in range(CHAIN):
                first = (bead * CHAIN + link) * 3
                pth[first : first + 3, at] = z[link]
            vel.append(q * jnp.exp(z[0] * -h) * inv)
        send1[p, 0:3, 0:chunk] = pos[0, :, at]
        send1[p, 3:6, 0:chunk] = pos[1, :, at]
        send1[p, 6:8, 0:chunk] = vel[0][0:2]
        for part in range(2):
            cut = slice(part * half, (part + 1) * half)
            to = slice(chunk, chunk + half)
            send1[p, 4 * part : 4 * part + 1, to] = vel[0][2:3, cut]
            send1[p, 4 * part + 1 : 4 * part + 4, to] = vel[1][:, cut]

    def exchange(out, got, ssem, rsem, off):
        p = ring(off)
        return pltpu.make_async_remote_copy(
            src_ref=out.at[p], dst_ref=got.at[me_b], send_sem=ssem.at[off], recv_sem=rsem.at[off],
            device_id=(p, me_s), device_id_type=MESH)

    def arrival(out, got, ssem, rsem, off):
        p = ring(-off)
        return pltpu.make_async_remote_copy(
            src_ref=out.at[p], dst_ref=got.at[p], send_sem=ssem.at[off], recv_sem=rsem.at[off],
            device_id=(p, me_s), device_id_type=MESH)

    def far_first(step):
        k = (step + 1) // 2
        return peers // 2 + jnp.where(lax.rem(step, 2) == 1, -k, k)

    def send_chunk(step, carry):
        off = far_first(step)
        chain(ring(off))
        exchange(send1, recv1, s1, r1, off).start()
        return carry

    lax.fori_loop(0, peers - 1, send_chunk, 0)
    chain(me_b)
    recv1[me_b] = send1[me_b]

    into[...] = jnp.full(into.shape, -1.0, f32)
    into[0:4, 0 : rows.shape[1]] = rows[...].astype(f32)
    listed = into[0:4]
    place = lax.broadcasted_iota(jnp.int32, (1, CAP), 1)
    for c in range(4):
        other = opposite[c]
        live = place < count[0, other]
        into[8 + c : 9 + c] = jnp.where(live, listed[other : other + 1], -1.0)
    landing = into[...].T

    def leave_map(n, carry):
        at = lanes(n * CAP, CAP)
        slot = (lax.broadcasted_iota(jnp.int32, (CAP, CAP), 0) + n * CAP).astype(f32)
        for c in range(4):
            gat[at, c * CAP : (c + 1) * CAP] = jnp.where(slot == listed[c : c + 1], 1.0, 0.0).astype(bf16)
        return carry

    lax.fori_loop(0, slots // CAP, leave_map, 0, unroll=2)

    pth[24:32] = jnp.zeros((8, slots), f32)
    pth[24:25] = types[...].astype(f32)

    def early_gather(n, total):
        at = lanes(n * chunk, chunk)
        x1, x2, x3 = split3(pth[0:24, at])
        left = jnp.concatenate([x1, x2, x3, pth[24:32, at]], axis=0).astype(bf16)
        return total + jnp.dot(left, gat[at, :], preferred_element_type=f32)

    got = lax.fori_loop(0, peers, early_gather, jnp.zeros((80, 4 * CAP), f32))
    early = got[0:24] + got[24:48] + got[48:72]

    def hop(out, got, ssem, rsem, c, to):
        return pltpu.make_async_remote_copy(
            src_ref=out.at[c], dst_ref=got.at[c], send_sem=ssem.at[c], recv_sem=rsem.at[c],
            device_id=(me_b, domain(to)), device_id_type=MESH)

    for c in range(4):
        e_out[c, 0:24] = early[:, c * CAP : (c + 1) * CAP]
        e_out[c, 24:32] = got[72:80, c * CAP : (c + 1) * CAP]
        hop(e_out, e_in, se, re, c, offsets[c]).start()

    def land_map(n, carry):
        at = lanes(n * CAP, CAP)
        slot = (lax.broadcasted_iota(jnp.int32, (CAP, CAP), 1) + n * CAP).astype(f32)
        for c in range(4):
            sca[c * CAP : (c + 1) * CAP, at] = jnp.where(slot == landing[:, 8 + c : 9 + c], 1.0, 0.0).astype(bf16)
        return carry

    lax.fori_loop(0, slots // CAP, land_map, 0, unroll=2)

    def take1(off, carry):
        arrival(send1, recv1, s1, r1, off).wait_recv()
        return carry

    lax.fori_loop(1, peers, take1, 0)
    size = peers * 8
    right = jnp.concatenate(
        [recv1[:, :, n * half : (n + 1) * half].reshape(size, half) for n in range(3)], axis=0)
    mixed = jnp.dot(bigm[...], right, preferred_element_type=f32, precision=lax.Precision.HIGHEST)
    for n in range(3):
        send2[:, :, n * half : (n + 1) * half] = mixed[n * size : (n + 1) * size].reshape(peers, 8, half)

    def send_mixed(step, carry):
        exchange(send2, recv2, s2, r2, far_first(step)).start()
        return carry

    lax.fori_loop(0, peers - 1, send_mixed, 0)
    recv2[me_b] = send2[me_b]

    for c in range(4):
        hop(e_out, e_in, se, re, c, -offsets[c]).wait_recv()
    x1, x2, x3 = split3(jnp.concatenate([e_in[c, 0:24] for c in range(4)], axis=1))
    kinds = jnp.concatenate([e_in[c, 24:32] for c in range(4)], axis=1)
    tag = lax.broadcasted_iota(jnp.int32, (8, 4 * CAP), 0)
    kinds = jnp.where(tag == 0, kinds, 1.0)
    early_left = jnp.concatenate([x1, x2, x3, kinds], axis=0).astype(bf16)

    def early_land(n, carry):
        at = lanes(n * 256, 256)
        new = jnp.dot(early_left, sca[:, at], preferred_element_type=f32)
        hit = new[73:74]
        mask[:, at] = hit
        merged = jnp.where(hit > 0.5, new[0:24] + new[24:48] + new[48:72], pth[0:24, at])
        for bead in range(2):
            for link in range(CHAIN):
                first = (bead * CHAIN + link) * 3
                tho[bead, link, :, at] = merged[first : first + 3]
        ext[1, 6:7, at] = jnp.where(hit > 0.5, new[72:73], pth[24:25, at])
        return carry

    ext[1, 7:8] = jnp.zeros((1, slots), f32)
    lax.fori_loop(0, slots // 256, early_land, 0, unroll=2)

    row_id = lax.broadcasted_iota(jnp.int32, (8, chunk), 0)

    def unpack(p, total):
        at = lanes(p * chunk, chunk)
        m = mass[:, at]
        main = recv2[p, :, 0:chunk]
        rest = recv2[p, :, chunk : chunk + half]
        top = jnp.where(row_id < 6, main, main * m)
        low = jnp.concatenate([rest[0:4] * m[:, 0:half], rest[4:8] * m[:, half:chunk]], axis=1)
        both = jnp.concatenate([top, low, jnp.zeros((4, chunk), f32)], axis=0)
        pd[:, at] = both
        left = jnp.concatenate(split3(both), axis=0).astype(bf16)
        return total + jnp.dot(left, gat[at, :], preferred_element_type=f32)

    total = unpack(me_b, jnp.zeros((48, 4 * CAP), f32))

    def take2(step, total):
        off = far_first(peers - 2 - step)
        arrival(send2, recv2, s2, r2, off).wait_recv()
        return unpack(ring(-off), total)

    total = lax.fori_loop(0, peers - 1, take2, total)
    late = total[0:16] + total[16:32] + total[32:48]
    late_row = lax.broadcasted_iota(jnp.int32, (16, CAP), 0)
    is_x = (late_row == 0) | (late_row == 3)
    for c in range(4):
        block = late[:, c * CAP : (c + 1) * CAP]
        l_out[c] = jnp.where(is_x, block - float(offsets[c]), block)
        hop(l_out, l_in, sl, rl, c, offsets[c]).start()

    for c in range(4):
        hop(l_out, l_in, sl, rl, c, -offsets[c]).wait_recv()
    late_left = jnp.concatenate(
        split3(jnp.concatenate([l_in[c] for c in range(4)], axis=1)), axis=0).astype(bf16)

    def late_land(n, carry):
        at = lanes(n * 256, 256)
        new = jnp.dot(late_left, sca[:, at], preferred_element_type=f32)
        merged = jnp.where(mask[:, at] > 0.5, new[0:16] + new[16:32] + new[32:48], pd[:, at])
        ext[1, 0:6, at] = merged[0:6]
        momo[0, :, at] = merged[6:9]
        momo[1, :, at] = merged[9:12]
        return carry

    width = slots // halo_parts

    def halo(side, part, to):
        cut = slice(part * width, (part + 1) * width)
        return pltpu.make_async_remote_copy(
            src_ref=ext.at[1, :, cut], dst_ref=ext.at[2 * side, :, cut],
            send_sem=sh.at[side, part], recv_sem=rh.at[side, part],
            device_id=(me_b, domain(to)), device_id_type=MESH)

    blocks = width // 256
    for part in range(halo_parts):
        lax.fori_loop(part * blocks, (part + 1) * blocks, late_land, 0, unroll=2)
        halo(0, part, 1).start()
        halo(1, part, -1).start()

    for part in range(halo_parts):
        halo(0, part, -1).wait_recv()
        halo(1, part, 1).wait_recv()

    def drain(off, carry):
        exchange(send1, recv1, s1, r1, off).wait_send()
        exchange(send2, recv2, s2, r2, off).wait_send()
        return carry

    lax.fori_loop(1, peers, drain, 0)
    for c in range(4):
        hop(e_out, e_in, se, re, c, offsets[c]).wait_send()
        hop(l_out, l_in, sl, rl, c, offsets[c]).wait_send()
    for part in range(halo_parts):
        halo(0, part, 1).wait_send()
        halo(1, part, -1).wait_send()


def front(peers, domains, pos, mom, thermo, types, masses, rows, count, bigm):
    slots = pos.shape[2]
    chunk = slots // peers
    packed = chunk + chunk // 2
    vm = pl.BlockSpec(memory_space=pltpu.VMEM)
    sm = pl.BlockSpec(memory_space=pltpu.SMEM)
    dma = pltpu.SemaphoreType.DMA
    shape = jax.ShapeDtypeStruct
    return pl.pallas_call(
        functools.partial(front_kernel, peers, domains),
        out_shape=(
            shape((3, 8, slots), f32),
            shape((2, 3, slots), f32),
            shape((2, CHAIN, 3, slots), f32),
        ),
        in_specs=[vm, vm, vm, vm, vm, vm, sm, vm],
        out_specs=(vm, vm, vm),
        scratch_shapes=[
            pltpu.VMEM((peers, 8, packed), f32),
            pltpu.VMEM((peers, 8, packed), f32),
            pltpu.VMEM((peers, 8, packed), f32),
            pltpu.VMEM((peers, 8, packed), f32),
            pltpu.VMEM((16, slots), f32),
            pltpu.VMEM((32, slots), f32),
            pltpu.VMEM((1, slots), f32),
            pltpu.VMEM((1, slots), f32),
            pltpu.VMEM((1, slots), f32),
            pltpu.VMEM((CAP, CAP), f32),
            pltpu.VMEM((slots, 4 * CAP), bf16),
            pltpu.VMEM((4 * CAP, slots), bf16),
            pltpu.VMEM((4, 32, CAP), f32),
            pltpu.VMEM((4, 32, CAP), f32),
            pltpu.VMEM((4, 16, CAP), f32),
            pltpu.VMEM((4, 16, CAP), f32),
            dma((peers,)), dma((peers,)), dma((peers,)), dma((peers,)),
            dma((4,)), dma((4,)), dma((4,)), dma((4,)),
            dma((2, halo_parts)), dma((2, halo_parts)),
        ],
        compiler_params=pltpu.CompilerParams(
            collective_id=0, has_side_effects=True, vmem_limit_bytes=48 * 2**20),
        name="front",
    )(pos, mom, thermo, types, masses, rows, count, bigm)


def force_kernel(
    tiles, count, ext, mom, thermo, table,
    force, momo, poso, kindo, tho,
    far, strength, near, moment, total, w0, w1, sem,
):
    slots = ext.shape[2]
    cells = slots // CAP
    keep = pltpu.make_async_copy(thermo, tho, sem)
    keep.start()
    rid = lax.broadcasted_iota(jnp.int32, (8, CAP), 0)
    comp = lax.rem(rid, 3)
    lane = lax.broadcasted_iota(jnp.int32, (CAP, CAP), 1).astype(f32)
    subl = lax.broadcasted_iota(jnp.int32, (CAP, CAP), 0).astype(f32)

    def cell_at(c):
        return pl.ds(pl.multiple_of(c * CAP, CAP), CAP)

    def scaled(dom, c):
        block = ext[dom, :, cell_at(c)]
        middle = jnp.where(comp == 0, centre[0] - (dom - 1.0), jnp.where(comp == 1, centre[1], centre[2]))
        u = (block - middle) * spread
        sq = u * u * -0.5
        n0 = sq[0:1] + sq[1:2] + sq[2:3]
        n1 = sq[3:4] + sq[4:5] + sq[5:6]
        return block, u, n0, n1, jnp.where(rid < 6, u, jnp.where(rid == 6, n0, n1))

    def prepare_far(dom):
        def body(c, carry):
            block, u, n0, n1, x = scaled(dom, c)
            x1, x2, x3 = split3(x)
            kind = jnp.broadcast_to(block[6:7], (8, CAP))
            rows = jnp.concatenate(
                [x1, x1, x2, x2, x1, x3, jnp.ones_like(x1), kind, jnp.zeros((64, CAP), f32)], axis=0)
            turned = rows.T
            cell = dom * cells + c
            far[cell, :, 128:256] = turned.astype(bf16)
            far[cell, :, 0:128] = jnp.where(turned[:, 56:57] == lane, 1.0, 0.0).astype(bf16)
            one = jnp.ones((1, CAP), f32)
            zero = jnp.zeros((1, CAP), f32)
            q = jnp.concatenate(
                [one, x1[0:3], x2[0:3], zero, one, x1[3:6], x2[3:6], zero], axis=0).astype(bf16)
            moment[cell] = jnp.concatenate([q, q], axis=1)
            return carry

        lax.fori_loop(0, cells, body, 0, unroll=prep_unroll)

    for dom in range(3):
        prepare_far(dom)

    def prepare_near(c, carry):
        block, u, n0, n1, x = scaled(1, c)
        x1, x2, x3 = split3(x)
        kind = jnp.broadcast_to(block[6:7], (CAP, CAP))
        onehot = jnp.where(kind == subl, 1.0, 0.0).astype(bf16)
        strength[c] = jnp.dot(table[...], onehot, preferred_element_type=f32).astype(bf16)
        for bead in range(2):
            mine = (rid >= 3 * bead) & (rid < 3 * bead + 3)
            unit = jnp.where(rid == 6 + bead, 1.0, 0.0)
            m1, m2, m3 = split3((n0 if bead == 0 else n1) + log_scale)
            norms = jnp.where(rid == 0, m1, jnp.where(rid == 1, m2, jnp.where(rid == 2, m3, 0.0)))
            y1, y2, y3 = (jnp.where(mine, v, 0.0) for v in (x1, x2, x3))
            z1 = jnp.where(mine, x1, unit)
            rows = jnp.concatenate([z1, y2, z1, y2, y3, z1, norms, jnp.zeros_like(norms)], axis=0)
            near[c, :, bead * CAP : (bead + 1) * CAP] = rows.astype(bf16)
        return carry

    lax.fori_loop(0, cells, prepare_near, 0, unroll=prep_unroll)
    near[cells] = jnp.zeros(near.shape[1:], bf16)
    strength[cells] = jnp.zeros(strength.shape[1:], bf16)
    total[...] = jnp.zeros(total.shape, f32)
    w1[...] = jnp.zeros(w1.shape, bf16)
    live_tiles = count[0]
    last = tiles.shape[1] - 1

    def weigh(t, w, k):
        at = jnp.minimum(t, last)
        i = jnp.where(t < live_tiles, tiles[0, at], cells)
        j = tiles[1, at]
        s = jnp.dot(far[j, :, 0:128], strength[i], preferred_element_type=f32)
        e = jnp.dot(far[j, :, 128:192], near[i], preferred_element_type=f32)
        for bead in range(2):
            cut = slice(bead * CAP, (bead + 1) * CAP)
            weight = s * jnp.exp2(e[:, cut])
            high = weight.astype(bf16)
            w[k, 0:CAP, cut] = high
            w[k, CAP : 2 * CAP, cut] = (weight - high.astype(f32)).astype(bf16)

    def gather_force(t, w, k):
        at = jnp.clip(t, 0, last)
        i = jnp.where((t >= 0) & (t < live_tiles), tiles[0, at], cells)
        f = jnp.dot(moment[tiles[1, at]], w[k], preferred_element_type=f32)
        total[i, 0] += f[0:8, 0:CAP]
        total[i, 1] += f[8:16, CAP : 2 * CAP]

    def step(b, carry):
        base = b * 2 * batch
        for k in range(batch):
            weigh(base + k, w0, k)
            gather_force(base - batch + k, w1, k)
        for k in range(batch):
            weigh(base + batch + k, w1, k)
            gather_force(base + k, w0, k)
        return carry

    steps = (live_tiles + 2 * batch - 1) // (2 * batch)
    lax.fori_loop(0, steps, step, 0)
    for k in range(batch):
        gather_force(steps * 2 * batch - batch + k, w1, k)

    def finish(c, carry):
        block, u, n0, n1, x = scaled(1, c)
        at = cell_at(c)
        for bead in range(2):
            r = total[c, bead]
            got = (u[3 * bead : 3 * bead + 3] * r[0:1] - r[1:4] - r[4:7]) * (1.0 / spread)
            force[bead, :, at] = got
            momo[bead, :, at] = mom[bead, :, at] + inner_step * got
            poso[bead, :, at] = block[3 * bead : 3 * bead + 3]
        kindo[:, at] = block[6:7].astype(jnp.int32)
        return carry

    lax.fori_loop(0, cells, finish, 0, unroll=prep_unroll)
    keep.wait()


def pair_forces(tiles, count, ext, mom, thermo, table):
    slots = ext.shape[2]
    cells = slots // CAP
    vm = pl.BlockSpec(memory_space=pltpu.VMEM)
    sm = pl.BlockSpec(memory_space=pltpu.SMEM)
    hbm = pl.BlockSpec(memory_space=pl.ANY)
    shape = jax.ShapeDtypeStruct
    beads = shape((2, 3, slots), f32)
    return pl.pallas_call(
        force_kernel,
        out_shape=(beads, beads, beads, shape((1, slots), jnp.int32), shape(thermo.shape, f32)),
        in_specs=[sm, sm, vm, vm, hbm, vm],
        out_specs=(vm, vm, vm, vm, hbm),
        scratch_shapes=[
            pltpu.VMEM((3 * cells, CAP, 256), bf16),
            pltpu.VMEM((cells + 1, CAP, CAP), bf16),
            pltpu.VMEM((cells + 1, 64, 256), bf16),
            pltpu.VMEM((3 * cells, 16, 256), bf16),
            pltpu.VMEM((cells + 1, 2, 8, CAP), f32),
            pltpu.VMEM((batch, 256, 256), bf16),
            pltpu.VMEM((batch, 256, 256), bf16),
            pltpu.SemaphoreType.DMA,
        ],
        compiler_params=pltpu.CompilerParams(vmem_limit_bytes=48 * 2**20),
        name="pair_forces",
    )(tiles, count, ext, mom, thermo, table)


def per_device(peers, domains, positions, momenta, thermostat, atom_types, masses, pair_table,
               tile_pairs, tile_count, move_rows, move_count):
    slots = positions.shape[2]
    ext, moved, thermo = front(
        peers, domains, positions, momenta, thermostat, atom_types.reshape(1, slots),
        masses.reshape(1, -1), move_rows[0], move_count, jnp.asarray(cycle_map(peers)))
    forces, momenta_out, positions_out, kinds, thermo_out = pair_forces(
        tile_pairs[0], tile_count, ext, moved, thermo, pair_table)
    return positions_out, momenta_out, thermo_out, forces, kinds.reshape(slots)


def solution(mesh):
    placed = (
        P("bead", None, "space"),
        P("bead", None, "space"),
        P("bead", None, None, "space"),
        P("space"),
        P(),
        P(),
        P("space", None, None),
        P("space"),
        P("space", None, None),
        P("space", None),
    )
    return jax.shard_map(
        functools.partial(per_device, mesh.shape["bead"], mesh.shape["space"]),
        mesh=mesh,
        in_specs=placed,
        out_specs=(
            P("bead", None, "space"),
            P("bead", None, "space"),
            P("bead", None, None, "space"),
            P("bead", None, "space"),
            P("space"),
        ),
        check_vma=False,
    )
```

time: 793 us -> 90 us (0.11)
  the two profiles are of different devices: /device:TPU:31 before, /device:TPU:5 now
where the time goes in v1:
time: 90 us; the launch traced here: 89.9 us
  Pallas kernels  82 us (91%)
  local copies, waits for them, and re-layouts  6.46 us (7%)
  between operations  1.46 us (2%)
    pallas_call x1, Pallas kernels, pair_forces(): pl.pallas_call(force_kernel, out_shape=(beads, beads, beads, shape((1, sl...  43.5 us
    pallas_call x1, Pallas kernels, front(): pl.pallas_call(functools.partial(front_kernel, peers, domains), out_shape...  38.4 us
    unnamed x23, local copies, waits for them, and re-layouts  6.46 us

profile of v1, /device:TPU:5, one launch (start us, length us, event | category | flops | bytes accessed | tf_op | source)
XLA Modules:
  0.0 89.9 jit_solution(12014827757477660546)
XLA Ops:
  0.6 0.0 copy-start.7
  1.3 1.0 %copy.16.pos = f32[2,3,6144]{2,1,0:T(4,128)S(1)} copy(f32[2,3,6144]{2,0,1:T(2,128)} %param.11) | data formatting | bytes 294912 | tf_op args[0]
  2.4 1.0 %copy.17.mom = f32[2,3,6144]{2,1,0:T(4,128)S(1)} copy(f32[2,3,6144]{2,0,1:T(2,128)} %param.12) | data formatting | bytes 294912 | tf_op args[1]
  3.4 0.0 copy-done.7
  3.4 0.0 copy-start
  3.4 0.0 copy-start.2
  3.4 0.0 copy-start.4
  3.4 0.0 copy-start.5
  3.4 0.0 copy-start.6
  3.5 0.4 copy.18.thermo
  3.9 0.5 copy-done
  4.3 0.0 copy-done.2
  4.3 0.0 copy-done.4
  4.3 0.0 copy-done.5
  4.3 0.0 copy-done.6
  4.3 0.0 copy-start.1
  4.4 0.0 copy-start.3
  4.4 38.4 %front.1 = (f32[3,8,6144]{2,1,0:T(8,128)S(1)}, f32[2,3,6144]{2,1,0:T(4,128)S(1)}, f32[2,4,3,6144]{3,2,1,0:T(4,128)S(1)}) custom-call(f32[2,3,6144]{2,1,0:T(4,128)S(1)} %copy.16.pos, f32[2,3,6144]{2,1,0:T(4,128)S(1)} %copy.17.mom, f32[2,4,3,6144]{3,2,1,0:T(4,128)S(1)} %copy.18.thermo, s32[1,6144]{1,0:T(1,128)S(1)} %bitcast.5, f32[1,128]{1,0:T(1,128)S(1)} %bitcast.8, ...), custom_call_target="tpu_custom_call" | custom-call | tf_op jit(solution)/shard_map/front/pallas_call | solution.py:352
  42.8 0.0 copy-done.1
  42.8 0.0 copy-done.3
  42.8 43.5 %pair_forces.1 = (f32[2,3,6144]{2,1,0:T(4,128)S(1)}, f32[2,3,6144]{2,1,0:T(4,128)S(1)}, f32[2,3,6144]{2,1,0:T(4,128)S(1)}, s32[1,6144]{1,0:T(1,128)}, f32[2,4,3,6144]{3,2,1,0:T(4,128)S(1)}) custom-call(s32[2,672]{1,0:T(2,128)S(1)} %bitcast.6, s32[1]{0:T(128)S(6)} %copy.23.count, f32[3,8,6144]{2,1,0:T(8,128)S(1)} %get-tuple-element.13.ext, ...), custom_call_target="tpu_custom_call" | custom-call | tf_op jit(solution)/shard_map/pair_forces/pallas_call | solution.py:521
  86.4 0.8 copy.19
  87.1 0.8 copy.20
  87.9 0.8 copy.22
  88.7 1.2 %copy.21 = f32[2,4,3,6144]{3,1,2,0:T(4,128)} copy(f32[2,4,3,6144]{3,2,1,0:T(4,128)S(1)} %get-tuple-element.23) | data formatting | bytes 1179648
Async XLA Ops:
  0.6 2.8 %copy-start.7 = (f32[2,4,3,6144]{3,1,2,0:T(4,128)S(1)}, f32[2,4,3,6144]{3,1,2,0:T(4,128)}, u32[]{:S(2)}) copy-start(f32[2,4,3,6144]{3,1,2,0:T(4,128)} %param.13) | copy-start | bytes 1769476
  3.4 0.9 %copy-start = (f32[192,192]{1,0:T(8,128)S(1)}, f32[192,192]{1,0:T(8,128)}, u32[]{:S(2)}) copy-start(f32[192,192]{1,0:T(8,128)} %constant.2.clone.bigm) | copy-start | bytes 442372
  3.4 0.9 %copy-start.2 = (s32[6144]{0:T(1024)S(1)}, s32[6144]{0:T(1024)}, u32[]{:S(2)}) copy-start(s32[6144]{0:T(1024)} %param.14) | copy-start | bytes 73732
  3.4 0.9 %copy-start.4 = (s32[1,4,96]{2,1,0:T(4,128)S(1)}, s32[1,4,96]{2,1,0:T(4,128)}, u32[]{:S(2)}) copy-start(s32[1,4,96]{2,1,0:T(4,128)} %param.19) | copy-start | bytes 4612
  3.4 0.9 %copy-start.5 = (f32[128]{0:T(128)S(1)}, f32[128]{0:T(128)}, u32[]{:S(2)}) copy-start(f32[128]{0:T(128)} %param.15) | copy-start | bytes 1540
  3.4 0.9 copy-start.6
  4.3 38.5 %copy-start.1 = (bf16[128,128]{1,0:T(8,128)(2,1)S(1)}, bf16[128,128]{1,0:T(8,128)(2,1)}, u32[]{:S(2)}) copy-start(bf16[128,128]{1,0:T(8,128)(2,1)} %table.1) | copy-start | bytes 98308
  4.4 38.5 %copy-start.3 = (s32[1,2,672]{2,1,0:T(2,128)S(1)}, s32[1,2,672]{2,1,0:T(2,128)}, u32[]{:S(2)}) copy-start(s32[1,2,672]{2,1,0:T(2,128)} %param.17) | copy-start | bytes 16132

commit v2 on v1

--- a/solution.py
+++ b/solution.py
@@ -29,8 +29,8 @@
 spread = math.sqrt(1.0 / (reach2 * math.log(2.0)))
 log_scale = math.log2(1.0 / (reach2 * NBEADS))
 centre = (0.5, 4.0, 3.0)
-batch = 8
-prep_unroll = 8
+batch = 16
+prep_unroll = 16
 halo_parts = 4
 
 
@@ -56,7 +56,7 @@
     big = np.zeros((3 * size, 3 * size))
 
     def place(p, kind, bead, comp, half):
-        row = (kind * per + bead) * 3 + comp
+        row = (kind * 3 + comp) * per + bead
         if row < 8:
             return half * size + p * 8 + row
         return 2 * size + p * 8 + half * 4 + row - 8
@@ -123,27 +123,24 @@
         at = lanes(p * chunk, chunk)
         inv = inverse[:, at]
         h = 0.5 * outer_step
-        vel = []
-        for bead in range(2):
-            z = [thermo[bead, link, :, at] for link in range(CHAIN)]
-            q = mom[bead, :, at]
-            old = [q * q * inv * (1.0 / chain_mass)] + [v * v for v in z[:-1]]
-            z[3] = z[3] + h * (old[3] - thermal / chain_mass)
-            for link in (2, 1, 0):
-                drive = old[link] - thermal / chain_mass
-                z[link] = z[link] * jnp.exp(z[link + 1] * -h) + h * drive
-            for link in range(CHAIN):
-                first = (bead * CHAIN + link) * 3
-                pth[first : first + 3, at] = z[link]
-            vel.append(q * jnp.exp(z[0] * -h) * inv)
-        send1[p, 0:3, 0:chunk] = pos[0, :, at]
-        send1[p, 3:6, 0:chunk] = pos[1, :, at]
-        send1[p, 6:8, 0:chunk] = vel[0][0:2]
+        q = jnp.concatenate([mom[n, :, at] for n in range(3)], axis=0)
+        z = [
+            jnp.concatenate([thermo[b, n, link : link + 1, at] for n in range(3) for b in range(2)], axis=0)
+            for link in range(CHAIN)
+        ]
+        old = [q * q * inv * (1.0 / chain_mass)] + [v * v for v in z[:-1]]
+        z[3] = z[3] + h * (old[3] - thermal / chain_mass)
+        for link in (2, 1, 0):
+            drive = old[link] - thermal / chain_mass
+            z[link] = z[link] * jnp.exp(z[link + 1] * -h) + h * drive
+        for link in range(CHAIN):
+            pth[6 * link : 6 * link + 6, at] = z[link]
+        vel = q * jnp.exp(z[0] * -h) * inv
+        for n in range(3):
+            send1[p, 2 * n : 2 * n + 2, 0:chunk] = pos[n, :, at]
+        send1[p, 6:8, 0:chunk] = vel[0:2]
         for part in range(2):
-            cut = slice(part * half, (part + 1) * half)
-            to = slice(chunk, chunk + half)
-            send1[p, 4 * part : 4 * part + 1, to] = vel[0][2:3, cut]
-            send1[p, 4 * part + 1 : 4 * part + 4, to] = vel[1][:, cut]
+            send1[p, 4 * part : 4 * part + 4, chunk : chunk + half] = vel[2:6, part * half : (part + 1) * half]
 
     def exchange(out, got, ssem, rsem, off):
         p = ring(off)
@@ -255,9 +252,10 @@
         mask[:, at] = hit
         merged = jnp.where(hit > 0.5, new[0:24] + new[24:48] + new[48:72], pth[0:24, at])
         for bead in range(2):
-            for link in range(CHAIN):
-                first = (bead * CHAIN + link) * 3
-                tho[bead, link, :, at] = merged[first : first + 3]
+            for n in range(3):
+                for link in range(CHAIN):
+                    first = 6 * link + 2 * n + bead
+                    tho[bead, n, link : link + 1, at] = merged[first : first + 1]
         ext[1, 6:7, at] = jnp.where(hit > 0.5, new[72:73], pth[24:25, at])
         return carry
 
@@ -288,7 +286,7 @@
     total = lax.fori_loop(0, peers - 1, take2, total)
     late = total[0:16] + total[16:32] + total[32:48]
     late_row = lax.broadcasted_iota(jnp.int32, (16, CAP), 0)
-    is_x = (late_row == 0) | (late_row == 3)
+    is_x = late_row < 2
     for c in range(4):
         block = late[:, c * CAP : (c + 1) * CAP]
         l_out[c] = jnp.where(is_x, block - float(offsets[c]), block)
@@ -304,8 +302,8 @@
         new = jnp.dot(late_left, sca[:, at], preferred_element_type=f32)
         merged = jnp.where(mask[:, at] > 0.5, new[0:16] + new[16:32] + new[32:48], pd[:, at])
         ext[1, 0:6, at] = merged[0:6]
-        momo[0, :, at] = merged[6:9]
-        momo[1, :, at] = merged[9:12]
+        for n in range(3):
+            momo[n, :, at] = merged[6 + 2 * n : 8 + 2 * n]
         return carry
 
     width = slots // halo_parts
@@ -353,8 +351,8 @@
         functools.partial(front_kernel, peers, domains),
         out_shape=(
             shape((3, 8, slots), f32),
-            shape((2, 3, slots), f32),
-            shape((2, CHAIN, 3, slots), f32),
+            shape((3, 2, slots), f32),
+            shape((2, 3, CHAIN, slots), f32),
         ),
         in_specs=[vm, vm, vm, vm, vm, vm, sm, vm],
         out_specs=(vm, vm, vm),
@@ -388,45 +386,42 @@
 def force_kernel(
     tiles, count, ext, mom, thermo, table,
     force, momo, poso, kindo, tho,
-    far, strength, near, moment, total, w0, w1, sem,
+    far, near, strength, moment, total, w0, w1, sem,
 ):
     slots = ext.shape[2]
     cells = slots // CAP
     keep = pltpu.make_async_copy(thermo, tho, sem)
     keep.start()
     rid = lax.broadcasted_iota(jnp.int32, (8, CAP), 0)
-    comp = lax.rem(rid, 3)
-    lane = lax.broadcasted_iota(jnp.int32, (CAP, CAP), 1).astype(f32)
+    comp = rid // 2
+    parity = lax.rem(rid, 2)
     subl = lax.broadcasted_iota(jnp.int32, (CAP, CAP), 0).astype(f32)
 
     def cell_at(c):
         return pl.ds(pl.multiple_of(c * CAP, CAP), CAP)
 
-    def scaled(dom, c):
+    def scaled(dom, c, extra):
         block = ext[dom, :, cell_at(c)]
         middle = jnp.where(comp == 0, centre[0] - (dom - 1.0), jnp.where(comp == 1, centre[1], centre[2]))
         u = (block - middle) * spread
         sq = u * u * -0.5
-        n0 = sq[0:1] + sq[1:2] + sq[2:3]
-        n1 = sq[3:4] + sq[4:5] + sq[5:6]
-        return block, u, n0, n1, jnp.where(rid < 6, u, jnp.where(rid == 6, n0, n1))
+        n = sq[0:2] + sq[2:4] + sq[4:6] + extra
+        return block, jnp.concatenate([u[0:6], n], axis=0)
 
     def prepare_far(dom):
         def body(c, carry):
-            block, u, n0, n1, x = scaled(dom, c)
+            block, x = scaled(dom, c, 0.0)
             x1, x2, x3 = split3(x)
-            kind = jnp.broadcast_to(block[6:7], (8, CAP))
-            rows = jnp.concatenate(
-                [x1, x1, x2, x2, x1, x3, jnp.ones_like(x1), kind, jnp.zeros((64, CAP), f32)], axis=0)
-            turned = rows.T
+            z1 = jnp.where(rid < 6, x1, 1.0)
+            z2 = jnp.where(rid < 6, x2, 1.0)
             cell = dom * cells + c
-            far[cell, :, 128:256] = turned.astype(bf16)
-            far[cell, :, 0:128] = jnp.where(turned[:, 56:57] == lane, 1.0, 0.0).astype(bf16)
-            one = jnp.ones((1, CAP), f32)
-            zero = jnp.zeros((1, CAP), f32)
-            q = jnp.concatenate(
-                [one, x1[0:3], x2[0:3], zero, one, x1[3:6], x2[3:6], zero], axis=0).astype(bf16)
-            moment[cell] = jnp.concatenate([q, q], axis=1)
+            kind = jnp.broadcast_to(block[6:7], (CAP, CAP))
+            rows = jnp.concatenate([x1, x2, x3, z1, z2, z1, jnp.zeros((80, CAP), f32)], axis=0)
+            far[cell, :, 0:CAP] = jnp.where(kind == subl, 1.0, 0.0).astype(bf16).T
+            far[cell, :, CAP : 2 * CAP] = rows.astype(bf16).T
+            q = jnp.concatenate([z1, jnp.where(rid < 6, x2, 0.0)], axis=0).astype(bf16)
+            moment[cell, :, 0:CAP] = q
+            moment[cell, :, CAP : 2 * CAP] = q
             return carry
 
         lax.fori_loop(0, cells, body, 0, unroll=prep_unroll)
@@ -435,20 +430,19 @@
         prepare_far(dom)
 
     def prepare_near(c, carry):
-        block, u, n0, n1, x = scaled(1, c)
+        block, x = scaled(1, c, log_scale)
         x1, x2, x3 = split3(x)
         kind = jnp.broadcast_to(block[6:7], (CAP, CAP))
         onehot = jnp.where(kind == subl, 1.0, 0.0).astype(bf16)
         strength[c] = jnp.dot(table[...], onehot, preferred_element_type=f32).astype(bf16)
         for bead in range(2):
-            mine = (rid >= 3 * bead) & (rid < 3 * bead + 3)
-            unit = jnp.where(rid == 6 + bead, 1.0, 0.0)
-            m1, m2, m3 = split3((n0 if bead == 0 else n1) + log_scale)
-            norms = jnp.where(rid == 0, m1, jnp.where(rid == 1, m2, jnp.where(rid == 2, m3, 0.0)))
-            y1, y2, y3 = (jnp.where(mine, v, 0.0) for v in (x1, x2, x3))
-            z1 = jnp.where(mine, x1, unit)
-            rows = jnp.concatenate([z1, y2, z1, y2, y3, z1, norms, jnp.zeros_like(norms)], axis=0)
-            near[c, :, bead * CAP : (bead + 1) * CAP] = rows.astype(bf16)
+            mine = (rid < 6) & (parity == bead)
+            norm = rid == 6 + bead
+            y1 = jnp.where(mine, x1, jnp.where(norm, 1.0, 0.0))
+            y12 = jnp.where(mine, x2, jnp.where(norm, x1, 0.0))
+            y2 = jnp.where(mine | norm, x2, 0.0)
+            y3 = jnp.where(mine | norm, x3, 0.0)
+            near[c, :, bead * CAP : (bead + 1) * CAP] = jnp.concatenate([y1, y1, y1, y12, y2, y3], axis=0).astype(bf16)
         return carry
 
     lax.fori_loop(0, cells, prepare_near, 0, unroll=prep_unroll)
@@ -458,13 +452,14 @@
     w1[...] = jnp.zeros(w1.shape, bf16)
     live_tiles = count[0]
     last = tiles.shape[1] - 1
+    even = parity == 0
 
     def weigh(t, w, k):
         at = jnp.minimum(t, last)
         i = jnp.where(t < live_tiles, tiles[0, at], cells)
         j = tiles[1, at]
-        s = jnp.dot(far[j, :, 0:128], strength[i], preferred_element_type=f32)
-        e = jnp.dot(far[j, :, 128:192], near[i], preferred_element_type=f32)
+        s = jnp.dot(far[j, :, 0:CAP], strength[i], preferred_element_type=f32)
+        e = jnp.dot(far[j, :, CAP : CAP + 48], near[i], preferred_element_type=f32)
         for bead in range(2):
             cut = slice(bead * CAP, (bead + 1) * CAP)
             weight = s * jnp.exp2(e[:, cut])
@@ -476,8 +471,8 @@
         at = jnp.clip(t, 0, last)
         i = jnp.where((t >= 0) & (t < live_tiles), tiles[0, at], cells)
         f = jnp.dot(moment[tiles[1, at]], w[k], preferred_element_type=f32)
-        total[i, 0] += f[0:8, 0:CAP]
-        total[i, 1] += f[8:16, CAP : 2 * CAP]
+        f = f[0:8] + f[8:16]
+        total[i] += jnp.where(even, f[:, 0:CAP], f[:, CAP : 2 * CAP])
 
     def step(b, carry):
         base = b * 2 * batch
@@ -495,14 +490,15 @@
         gather_force(steps * 2 * batch - batch + k, w1, k)
 
     def finish(c, carry):
-        block, u, n0, n1, x = scaled(1, c)
+        block, x = scaled(1, c, 0.0)
         at = cell_at(c)
-        for bead in range(2):
-            r = total[c, bead]
-            got = (u[3 * bead : 3 * bead + 3] * r[0:1] - r[1:4] - r[4:7]) * (1.0 / spread)
-            force[bead, :, at] = got
-            momo[bead, :, at] = mom[bead, :, at] + inner_step * got
-            poso[bead, :, at] = block[3 * bead : 3 * bead + 3]
+        r = total[c]
+        got = (x * jnp.where(even, r[6:7], r[7:8]) - r) * (1.0 / spread)
+        for n in range(3):
+            pair = got[2 * n : 2 * n + 2]
+            force[n, :, at] = pair
+            momo[n, :, at] = mom[n, :, at] + inner_step * pair
+            poso[n, :, at] = block[2 * n : 2 * n + 2]
         kindo[:, at] = block[6:7].astype(jnp.int32)
         return carry
 
@@ -517,7 +513,7 @@
     sm = pl.BlockSpec(memory_space=pltpu.SMEM)
     hbm = pl.BlockSpec(memory_space=pl.ANY)
     shape = jax.ShapeDtypeStruct
-    beads = shape((2, 3, slots), f32)
+    beads = shape((3, 2, slots), f32)
     return pl.pallas_call(
         force_kernel,
         out_shape=(beads, beads, beads, shape((1, slots), jnp.int32), shape(thermo.shape, f32)),
@@ -525,10 +521,10 @@
         out_specs=(vm, vm, vm, vm, hbm),
         scratch_shapes=[
             pltpu.VMEM((3 * cells, CAP, 256), bf16),
+            pltpu.VMEM((cells + 1, 48, 256), bf16),
             pltpu.VMEM((cells + 1, CAP, CAP), bf16),
-            pltpu.VMEM((cells + 1, 64, 256), bf16),
             pltpu.VMEM((3 * cells, 16, 256), bf16),
-            pltpu.VMEM((cells + 1, 2, 8, CAP), f32),
+            pltpu.VMEM((cells + 1, 8, CAP), f32),
             pltpu.VMEM((batch, 256, 256), bf16),
             pltpu.VMEM((batch, 256, 256), bf16),
             pltpu.SemaphoreType.DMA,
@@ -542,11 +538,14 @@
                tile_pairs, tile_count, move_rows, move_count):
     slots = positions.shape[2]
     ext, moved, thermo = front(
-        peers, domains, positions, momenta, thermostat, atom_types.reshape(1, slots),
+        peers, domains, positions.transpose(1, 0, 2), momenta.transpose(1, 0, 2),
+        thermostat.transpose(0, 2, 1, 3), atom_types.reshape(1, slots),
         masses.reshape(1, -1), move_rows[0], move_count, jnp.asarray(cycle_map(peers)))
     forces, momenta_out, positions_out, kinds, thermo_out = pair_forces(
         tile_pairs[0], tile_count, ext, moved, thermo, pair_table)
-    return positions_out, momenta_out, thermo_out, forces, kinds.reshape(slots)
+    return (
+        positions_out.transpose(1, 0, 2), momenta_out.transpose(1, 0, 2),
+        thermo_out.transpose(0, 2, 1, 3), forces.transpose(1, 0, 2), kinds.reshape(slots))
 
 
 def solution(mesh):

time: 90 us -> 79.6 us (0.88)
  the two profiles are of different devices: /device:TPU:5 before, /device:TPU:4 now
where the time goes in v2:
time: 79.6 us; the launch traced here: 79.4 us
  Pallas kernels  72.8 us (91%)
  local copies, waits for them, and re-layouts  5.22 us (7%)
  between operations  1.34 us (2%)
    pallas_call x1, Pallas kernels, front(): pl.pallas_call(functools.partial(front_kernel, peers, domains), out_shape...  38.7 us
    pallas_call x1, Pallas kernels, pair_forces(): pl.pallas_call(force_kernel, out_shape=(beads, beads, beads, shape((1, sl...  34.1 us
    unnamed x20, local copies, waits for them, and re-layouts  5.22 us

profile of v2, /device:TPU:4, one launch (start us, length us, event | category | flops | bytes accessed | tf_op | source)
XLA Modules:
  0.0 79.4 jit_solution(12643173099825883685)
XLA Ops:
  1.3 0.0 copy-start.7
  1.3 0.0 copy-start.8
  1.3 0.0 copy-start.9
  1.3 0.7 copy-done.7
  2.0 0.0 copy-done.8
  2.0 0.0 copy-done.9
  2.0 0.0 copy-start
  2.0 1.1 %copy-done = f32[2,4,3,6144]{3,1,2,0:T(4,128)S(1)} copy-done((f32[2,4,3,6144]{3,1,2,0:T(4,128)S(1)}, f32[2,4,3,6144]{3,1,2,0:T(4,128)}, u32[]{:S(2)}) %copy-start) | copy-done | bytes 589848
  3.0 0.0 copy-start.1
  3.0 0.9 %copy-done.1 = f32[192,192]{1,0:T(8,128)S(1)} copy-done((f32[192,192]{1,0:T(8,128)S(1)}, f32[192,192]{1,0:T(8,128)}, u32[]{:S(2)}) %copy-start.1) | copy-done | bytes 147480
  4.0 0.0 copy-start.2
  4.0 0.9 %copy-done.2 = f32[2,3,6144]{2,0,1:T(2,128)S(1)} copy-done((f32[2,3,6144]{2,0,1:T(2,128)S(1)}, f32[2,3,6144]{2,0,1:T(2,128)}, u32[]{:S(2)}) %copy-start.2) | copy-done | bytes 147480
  4.9 0.0 copy-start.3
  4.9 0.9 %copy-done.3 = f32[2,3,6144]{2,0,1:T(2,128)S(1)} copy-done((f32[2,3,6144]{2,0,1:T(2,128)S(1)}, f32[2,3,6144]{2,0,1:T(2,128)}, u32[]{:S(2)}) %copy-start.3) | copy-done | bytes 147480
  5.8 0.0 copy-start.5
  5.8 0.7 copy-done.5
  6.5 0.0 copy-start.4
  6.5 0.0 copy-start.6
  6.5 38.7 %front.1 = (f32[3,8,6144]{2,1,0:T(8,128)S(1)}, f32[3,2,6144]{2,1,0:T(2,128)S(1)}, f32[2,3,4,6144]{3,2,1,0:T(4,128)S(1)}) custom-call(f32[3,2,6144]{2,1,0:T(2,128)S(1)} %bitcast.13, f32[3,2,6144]{2,1,0:T(2,128)S(1)} %bitcast.14, f32[2,3,4,6144]{3,2,1,0:T(4,128)S(1)} %bitcast.12, s32[1,6144]{1,0:T(1,128)S(1)} %bitcast.15, f32[1,128]{1,0:T(1,128)S(1)} %bitcast.18, ...), custom_call_target="tpu_custom_call" | custom-call | tf_op jit(solution)/shard_map/front/pallas_call | solution.py:350
  45.2 0.0 copy-done.4
  45.2 0.0 copy-done.6
  45.2 34.1 %pair_forces.1 = (f32[3,2,6144]{2,1,0:T(2,128)}, f32[3,2,6144]{2,1,0:T(2,128)}, f32[3,2,6144]{2,1,0:T(2,128)}, s32[1,6144]{1,0:T(1,128)}, f32[2,3,4,6144]{3,2,1,0:T(4,128)}) custom-call(s32[2,672]{1,0:T(2,128)S(1)} %bitcast.16, s32[1]{0:T(128)S(6)} %copy.16.count, f32[3,8,6144]{2,1,0:T(8,128)S(1)} %get-tuple-element.13.ext, ...), custom_call_target="tpu_custom_call" | custom-call | tf_op jit(solution)/shard_map/pair_forces/pallas_call | solution.py:517
Async XLA Ops:
  1.3 0.7 copy-start.7
  1.3 0.7 copy-start.8
  1.3 0.7 copy-start.9
  2.0 1.1 %copy-start = (f32[2,4,3,6144]{3,1,2,0:T(4,128)S(1)}, f32[2,4,3,6144]{3,1,2,0:T(4,128)}, u32[]{:S(2)}) copy-start(f32[2,4,3,6144]{3,1,2,0:T(4,128)} %param.13) | copy-start | bytes 1769476
  3.0 0.9 %copy-start.1 = (f32[192,192]{1,0:T(8,128)S(1)}, f32[192,192]{1,0:T(8,128)}, u32[]{:S(2)}) copy-start(f32[192,192]{1,0:T(8,128)} %constant.2.clone.bigm) | copy-start | bytes 442372
  4.0 0.9 %copy-start.2 = (f32[2,3,6144]{2,0,1:T(2,128)S(1)}, f32[2,3,6144]{2,0,1:T(2,128)}, u32[]{:S(2)}) copy-start(f32[2,3,6144]{2,0,1:T(2,128)} %param.11) | copy-start | bytes 442372
  4.9 0.9 %copy-start.3 = (f32[2,3,6144]{2,0,1:T(2,128)S(1)}, f32[2,3,6144]{2,0,1:T(2,128)}, u32[]{:S(2)}) copy-start(f32[2,3,6144]{2,0,1:T(2,128)} %param.12) | copy-start | bytes 442372
  5.8 0.7 copy-start.5
  6.5 38.7 %copy-start.4 = (bf16[128,128]{1,0:T(8,128)(2,1)S(1)}, bf16[128,128]{1,0:T(8,128)(2,1)}, u32[]{:S(2)}) copy-start(bf16[128,128]{1,0:T(8,128)(2,1)} %table.1) | copy-start | bytes 98308
  6.5 38.7 %copy-start.6 = (s32[1,2,672]{2,1,0:T(2,128)S(1)}, s32[1,2,672]{2,1,0:T(2,128)}, u32[]{:S(2)}) copy-start(s32[1,2,672]{2,1,0:T(2,128)} %param.17) | copy-start | bytes 16132

commit v3 on v2

--- a/solution.py
+++ b/solution.py
@@ -31,7 +31,6 @@
 centre = (0.5, 4.0, 3.0)
 batch = 16
 prep_unroll = 16
-halo_parts = 4
 
 
 def split3(x):
@@ -70,16 +69,24 @@
                             to = place(j // per, kind, j % per, comp, half)
                             fro = place(i // per, kind2, i % per, comp, half)
                             big[to, fro] = maps[kind][kind2][j, i]
-    return big.astype(np.float32)
+    small = np.zeros((3, size, size))
+    for n, m in enumerate((mc, mb, ms)):
+        for comp in range(3):
+            for j in range(NBEADS):
+                for i in range(NBEADS):
+                    to = j // per * 8 + comp * per + j % per
+                    small[n, to, i // per * 8 + comp * per + i % per] = m[j, i]
+    return big.astype(np.float32), small.reshape(3 * size, size).astype(np.float32)
 
 
 def front_kernel(
     peers, domains,
-    pos, mom, thermo, types, masses, rows, count, bigm,
+    pos_in, mom_in, thermo_in, types_in, masses_in, rows_in, count_in, big_in, small_in,
     ext, momo, tho,
-    send1, recv1, send2, recv2, pd, pth, mass, mask, inverse, into, gat, sca,
-    e_out, e_in, l_out, l_in,
-    s1, r1, s2, r2, se, re, sl, rl, sh, rh,
+    pos, mom, thermo, types, masses, rows, count, bigm, smallm,
+    send1, recv1, send2, recv2, pth, mass, mask, into, picked, gat, sca,
+    mig1, got1, mig2, got2, scale, e_out, e_in,
+    load, s1, r1, s2, r2, sm1, rm1, sm2, rm2, se, re, sh, rh,
 ):
     slots = pos.shape[2]
     chunk = slots // peers
@@ -93,8 +100,18 @@
     def domain(off):
         return lax.rem(me_s + off + domains, domains)
 
-    def lanes(start, size, unit=128):
-        return pl.ds(pl.multiple_of(start, unit), size)
+    def lanes(start, size):
+        return pl.ds(pl.multiple_of(start, CAP), size)
+
+    def class_offset(c):
+        return (1 + c // 2) * (1 - 2 * (c % 2))
+
+    pairs = [
+        (types_in, types), (masses_in, masses), (pos_in, pos), (mom_in, mom), (thermo_in, thermo),
+        (rows_in, rows), (count_in, count), (big_in, bigm), (small_in, smallm)]
+    loads = [pltpu.make_async_copy(src, dst, load.at[n]) for n, (src, dst) in enumerate(pairs)]
+    for copy in loads:
+        copy.start()
 
     barrier = pltpu.get_barrier_semaphore()
     for off in range(1, peers):
@@ -102,27 +119,28 @@
     for off in offsets:
         pl.semaphore_signal(barrier, inc=1, device_id=(me_b, domain(off)), device_id_type=MESH)
 
+    for q in range(peers):
+        @pl.when(me_b != q)
+        def _():
+            pl.semaphore_signal(
+                barrier, inc=1, device_id=(q, domain(-class_offset(q // 2))), device_id_type=MESH)
+
+    for copy in loads[0:5]:
+        copy.wait()
     m1, m2, m3 = split3(masses[...])
     mass_rows = jnp.concatenate([m1, m2, m3, jnp.zeros((5, NTYPES), f32)], axis=0).astype(bf16)
     kind_iota = lax.broadcasted_iota(jnp.int32, (NTYPES, chunk), 0)
 
-    def find_mass(n, carry):
-        at = lanes(n * chunk, chunk)
-        kind = jnp.broadcast_to(types[:, at], (NTYPES, chunk))
-        onehot = jnp.where(kind == kind_iota, 1.0, 0.0).astype(bf16)
-        got = jnp.dot(mass_rows, onehot, preferred_element_type=f32)
-        found = got[0:1] + got[1:2] + got[2:3]
-        mass[:, at] = found
-        inverse[:, at] = 1.0 / found
-        return carry
-
-    lax.fori_loop(0, peers, find_mass, 0)
-    pl.semaphore_wait(barrier, peers - 1 + len(offsets))
-
     def chain(p):
         at = lanes(p * chunk, chunk)
-        inv = inverse[:, at]
+        kind = types[:, at]
+        onehot = jnp.where(jnp.broadcast_to(kind, (NTYPES, chunk)) == kind_iota, 1.0, 0.0).astype(bf16)
+        found = jnp.dot(mass_rows, onehot, preferred_element_type=f32)
+        found = found[0:1] + found[1:2] + found[2:3]
+        mass[:, at] = found
+        inv = 1.0 / found
         h = 0.5 * outer_step
+        place = jnp.concatenate([pos[n, :, at] for n in range(3)], axis=0)
         q = jnp.concatenate([mom[n, :, at] for n in range(3)], axis=0)
         z = [
             jnp.concatenate([thermo[b, n, link : link + 1, at] for n in range(3) for b in range(2)], axis=0)
@@ -136,8 +154,11 @@
         for link in range(CHAIN):
             pth[6 * link : 6 * link + 6, at] = z[link]
         vel = q * jnp.exp(z[0] * -h) * inv
-        for n in range(3):
-            send1[p, 2 * n : 2 * n + 2, 0:chunk] = pos[n, :, at]
+        none = jnp.zeros((2, chunk), f32)
+        pth[24:32, at] = jnp.concatenate([kind.astype(f32), found, none, none, none], axis=0)
+        pth[32:40, at] = jnp.concatenate([place, none], axis=0)
+        pth[40:48, at] = jnp.concatenate([vel, none], axis=0)
+        send1[p, 0:6, 0:chunk] = place
         send1[p, 6:8, 0:chunk] = vel[0:2]
         for part in range(2):
             send1[p, 4 * part : 4 * part + 4, chunk : chunk + half] = vel[2:6, part * half : (part + 1) * half]
@@ -158,46 +179,67 @@
         k = (step + 1) // 2
         return peers // 2 + jnp.where(lax.rem(step, 2) == 1, -k, k)
 
+    first = ring(far_first(0))
+    chain(first)
+    pl.semaphore_wait(barrier, 2 * (peers - 1) + len(offsets))
+    exchange(send1, recv1, s1, r1, far_first(0)).start()
+
     def send_chunk(step, carry):
         off = far_first(step)
         chain(ring(off))
         exchange(send1, recv1, s1, r1, off).start()
         return carry
 
-    lax.fori_loop(0, peers - 1, send_chunk, 0)
+    lax.fori_loop(1, peers - 1, send_chunk, 0)
     chain(me_b)
     recv1[me_b] = send1[me_b]
 
+    for copy in loads[5:]:
+        copy.wait()
     into[...] = jnp.full(into.shape, -1.0, f32)
     into[0:4, 0 : rows.shape[1]] = rows[...].astype(f32)
     listed = into[0:4]
-    place = lax.broadcasted_iota(jnp.int32, (1, CAP), 1)
+    spot = lax.broadcasted_iota(jnp.int32, (1, CAP), 1)
     for c in range(4):
         other = opposite[c]
-        live = place < count[0, other]
+        live = spot < jnp.broadcast_to(count[:, other : other + 1], (1, CAP))
         into[8 + c : 9 + c] = jnp.where(live, listed[other : other + 1], -1.0)
     landing = into[...].T
-
-    def leave_map(n, carry):
-        at = lanes(n * CAP, CAP)
-        slot = (lax.broadcasted_iota(jnp.int32, (CAP, CAP), 0) + n * CAP).astype(f32)
-        for c in range(4):
-            gat[at, c * CAP : (c + 1) * CAP] = jnp.where(slot == listed[c : c + 1], 1.0, 0.0).astype(bf16)
-        return carry
-
-    lax.fori_loop(0, slots // CAP, leave_map, 0, unroll=2)
-
-    pth[24:32] = jnp.zeros((8, slots), f32)
-    pth[24:25] = types[...].astype(f32)
-
-    def early_gather(n, total):
-        at = lanes(n * chunk, chunk)
-        x1, x2, x3 = split3(pth[0:24, at])
-        left = jnp.concatenate([x1, x2, x3, pth[24:32, at]], axis=0).astype(bf16)
-        return total + jnp.dot(left, gat[at, :], preferred_element_type=f32)
-
-    got = lax.fori_loop(0, peers, early_gather, jnp.zeros((80, 4 * CAP), f32))
-    early = got[0:24] + got[24:48] + got[48:72]
+    picked[...] = jnp.zeros(picked.shape, f32)
+    row_iota = lax.broadcasted_iota(jnp.int32, (CAP, CAP), 0)
+
+    def pick(n, carry):
+        for k in range(chunk // CAP):
+            slot = (row_iota + (n * chunk + k * CAP)).astype(f32)
+            for c in range(4):
+                gat[k * CAP : (k + 1) * CAP, c * CAP : (c + 1) * CAP] = jnp.where(
+                    slot == listed[c : c + 1], 1.0, 0.0).astype(bf16)
+        left = jnp.concatenate(split3(pth[:, lanes(n * chunk, chunk)]), axis=0).astype(bf16)
+        picked[...] += jnp.dot(left, gat[...], preferred_element_type=f32)
+        return carry
+
+    lax.fori_loop(0, peers, pick, 0)
+    leaving = picked[0:48] + picked[48:96] + picked[96:144]
+    low = lax.broadcasted_iota(jnp.int32, (8, CAP), 1) < CAP // 2
+
+    def swap(x):
+        return pltpu.roll(x, CAP // 2, 1)
+
+    for c in range(4):
+        cut = slice(c * CAP, (c + 1) * CAP)
+        place, vel = leaving[32:40, cut], leaving[40:48, cut]
+        mig1[2 * c] = jnp.where(low, place, swap(vel))
+        mig1[2 * c + 1] = jnp.where(low, swap(place), vel)
+        m = jnp.broadcast_to(leaving[25:26, cut], (8, CAP))
+        scale[2 * c] = jnp.where(low, 1.0, swap(m))
+        scale[2 * c + 1] = jnp.where(low, 1.0, m)
+
+    def send_leaving(step, carry):
+        exchange(mig1, got1, sm1, rm1, far_first(step)).start()
+        return carry
+
+    lax.fori_loop(0, peers - 1, send_leaving, 0)
+    got1[me_b] = mig1[me_b]
 
     def hop(out, got, ssem, rsem, c, to):
         return pltpu.make_async_remote_copy(
@@ -205,8 +247,7 @@
             device_id=(me_b, domain(to)), device_id_type=MESH)
 
     for c in range(4):
-        e_out[c, 0:24] = early[:, c * CAP : (c + 1) * CAP]
-        e_out[c, 24:32] = got[72:80, c * CAP : (c + 1) * CAP]
+        e_out[c] = leaving[0:32, c * CAP : (c + 1) * CAP]
         hop(e_out, e_in, se, re, c, offsets[c]).start()
 
     def land_map(n, carry):
@@ -230,10 +271,40 @@
     for n in range(3):
         send2[:, :, n * half : (n + 1) * half] = mixed[n * size : (n + 1) * size].reshape(peers, 8, half)
 
+    def take_leaving(off, carry):
+        arrival(mig1, got1, sm1, rm1, off).wait_recv()
+        return carry
+
+    lax.fori_loop(1, peers, take_leaving, 0)
+    turned = jnp.dot(
+        smallm[...], got1[...].reshape(size, CAP), preferred_element_type=f32,
+        precision=lax.Precision.HIGHEST)
+    low_all = lax.broadcasted_iota(jnp.int32, (size, CAP), 1) < CAP // 2
+    cross = swap(jnp.where(low_all, turned[size : 2 * size], turned[2 * size : 3 * size]))
+    mine = class_offset(me_b // 2)
+    is_x = (lax.broadcasted_iota(jnp.int32, (8, CAP), 0) < 2) & low
+    shift = jnp.where(is_x, mine.astype(f32), 0.0)
+    mig2[...] = (turned[0:size] + cross).reshape(peers, 8, CAP) * scale[me_b][None] - shift[None]
+
+    def deliver(p):
+        return pltpu.make_async_remote_copy(
+            src_ref=mig2.at[p], dst_ref=got2.at[me_b], send_sem=sm2.at[p], recv_sem=rm2.at[me_b],
+            device_id=(p, domain(mine)), device_id_type=MESH)
+
+    def delivered(q):
+        return pltpu.make_async_remote_copy(
+            src_ref=mig2.at[q], dst_ref=got2.at[q], send_sem=sm2.at[q], recv_sem=rm2.at[q],
+            device_id=(q, domain(-mine)), device_id_type=MESH)
+
+    def send_turned(p, carry):
+        deliver(p).start()
+        return carry
+
     def send_mixed(step, carry):
         exchange(send2, recv2, s2, r2, far_first(step)).start()
         return carry
 
+    lax.fori_loop(0, peers, send_turned, 0)
     lax.fori_loop(0, peers - 1, send_mixed, 0)
     recv2[me_b] = send2[me_b]
 
@@ -254,99 +325,91 @@
         for bead in range(2):
             for n in range(3):
                 for link in range(CHAIN):
-                    first = 6 * link + 2 * n + bead
-                    tho[bead, n, link : link + 1, at] = merged[first : first + 1]
+                    row = 6 * link + 2 * n + bead
+                    tho[bead, n, link : link + 1, at] = merged[row : row + 1]
         ext[1, 6:7, at] = jnp.where(hit > 0.5, new[72:73], pth[24:25, at])
         return carry
 
     ext[1, 7:8] = jnp.zeros((1, slots), f32)
     lax.fori_loop(0, slots // 256, early_land, 0, unroll=2)
 
-    row_id = lax.broadcasted_iota(jnp.int32, (8, chunk), 0)
-
-    def unpack(p, total):
+    def take_turned(q, carry):
+        delivered(q).wait_recv()
+        return carry
+
+    lax.fori_loop(0, peers, take_turned, 0)
+    came = [(got2[2 * c], got2[2 * c + 1]) for c in range(4)]
+    place = jnp.concatenate([jnp.where(low, even, swap(odd)) for even, odd in came], axis=1)
+    drift = jnp.concatenate([jnp.where(low, swap(even), odd) for even, odd in came], axis=1)
+    late_left = jnp.concatenate(
+        split3(jnp.concatenate([place, drift], axis=0)), axis=0).astype(bf16)
+
+    def halo(side, p, to):
+        cut = lanes(p * chunk, chunk)
+        return pltpu.make_async_remote_copy(
+            src_ref=ext.at[1, :, cut], dst_ref=ext.at[2 * side, :, cut],
+            send_sem=sh.at[side, p], recv_sem=rh.at[side, p],
+            device_id=(me_b, domain(to)), device_id_type=MESH)
+
+    def merge(p):
         at = lanes(p * chunk, chunk)
+        new = jnp.dot(late_left, sca[:, at], preferred_element_type=f32)
+        new = new[0:16] + new[16:32] + new[32:48]
+        hit = mask[:, at] > 0.5
         m = mass[:, at]
         main = recv2[p, :, 0:chunk]
         rest = recv2[p, :, chunk : chunk + half]
-        top = jnp.where(row_id < 6, main, main * m)
-        low = jnp.concatenate([rest[0:4] * m[:, 0:half], rest[4:8] * m[:, half:chunk]], axis=1)
-        both = jnp.concatenate([top, low, jnp.zeros((4, chunk), f32)], axis=0)
-        pd[:, at] = both
-        left = jnp.concatenate(split3(both), axis=0).astype(bf16)
-        return total + jnp.dot(left, gat[at, :], preferred_element_type=f32)
-
-    total = unpack(me_b, jnp.zeros((48, 4 * CAP), f32))
-
-    def take2(step, total):
+        ext[1, 0:6, at] = jnp.where(hit, new[0:6], main[0:6])
+        halo(0, p, 1).start()
+        halo(1, p, -1).start()
+        drift = jnp.concatenate([main[6:8], jnp.concatenate([rest[0:4], rest[4:8]], axis=1)], axis=0)
+        drift = jnp.where(hit, new[8:14], drift * m)
+        for n in range(3):
+            momo[n, :, at] = drift[2 * n : 2 * n + 2]
+
+    merge(me_b)
+
+    def take2(step, carry):
         off = far_first(peers - 2 - step)
         arrival(send2, recv2, s2, r2, off).wait_recv()
-        return unpack(ring(-off), total)
-
-    total = lax.fori_loop(0, peers - 1, take2, total)
-    late = total[0:16] + total[16:32] + total[32:48]
-    late_row = lax.broadcasted_iota(jnp.int32, (16, CAP), 0)
-    is_x = late_row < 2
-    for c in range(4):
-        block = late[:, c * CAP : (c + 1) * CAP]
-        l_out[c] = jnp.where(is_x, block - float(offsets[c]), block)
-        hop(l_out, l_in, sl, rl, c, offsets[c]).start()
-
-    for c in range(4):
-        hop(l_out, l_in, sl, rl, c, -offsets[c]).wait_recv()
-    late_left = jnp.concatenate(
-        split3(jnp.concatenate([l_in[c] for c in range(4)], axis=1)), axis=0).astype(bf16)
-
-    def late_land(n, carry):
-        at = lanes(n * 256, 256)
-        new = jnp.dot(late_left, sca[:, at], preferred_element_type=f32)
-        merged = jnp.where(mask[:, at] > 0.5, new[0:16] + new[16:32] + new[32:48], pd[:, at])
-        ext[1, 0:6, at] = merged[0:6]
-        for n in range(3):
-            momo[n, :, at] = merged[6 + 2 * n : 8 + 2 * n]
-        return carry
-
-    width = slots // halo_parts
-
-    def halo(side, part, to):
-        cut = slice(part * width, (part + 1) * width)
-        return pltpu.make_async_remote_copy(
-            src_ref=ext.at[1, :, cut], dst_ref=ext.at[2 * side, :, cut],
-            send_sem=sh.at[side, part], recv_sem=rh.at[side, part],
-            device_id=(me_b, domain(to)), device_id_type=MESH)
-
-    blocks = width // 256
-    for part in range(halo_parts):
-        lax.fori_loop(part * blocks, (part + 1) * blocks, late_land, 0, unroll=2)
-        halo(0, part, 1).start()
-        halo(1, part, -1).start()
-
-    for part in range(halo_parts):
-        halo(0, part, -1).wait_recv()
-        halo(1, part, 1).wait_recv()
+        merge(ring(-off))
+        return carry
+
+    lax.fori_loop(0, peers - 1, take2, 0)
 
     def drain(off, carry):
         exchange(send1, recv1, s1, r1, off).wait_send()
         exchange(send2, recv2, s2, r2, off).wait_send()
+        exchange(mig1, got1, sm1, rm1, off).wait_send()
         return carry
 
     lax.fori_loop(1, peers, drain, 0)
     for c in range(4):
         hop(e_out, e_in, se, re, c, offsets[c]).wait_send()
-        hop(l_out, l_in, sl, rl, c, offsets[c]).wait_send()
-    for part in range(halo_parts):
-        halo(0, part, 1).wait_send()
-        halo(1, part, -1).wait_send()
-
-
-def front(peers, domains, pos, mom, thermo, types, masses, rows, count, bigm):
+
+    def take_halo(p, carry):
+        deliver(p).wait_send()
+        halo(0, p, 1).wait_send()
+        halo(1, p, -1).wait_send()
+        halo(0, p, -1).wait_recv()
+        halo(1, p, 1).wait_recv()
+        return carry
+
+    lax.fori_loop(0, peers, take_halo, 0)
+
+
+def front(peers, domains, pos, mom, thermo, types, masses, rows, count):
     slots = pos.shape[2]
     chunk = slots // peers
     packed = chunk + chunk // 2
+    bigm, smallm = (jnp.asarray(m) for m in cycle_map(peers))
+    args = (pos, mom, thermo, types, masses, rows, count, bigm, smallm)
     vm = pl.BlockSpec(memory_space=pltpu.VMEM)
-    sm = pl.BlockSpec(memory_space=pltpu.SMEM)
+    hbm = pl.BlockSpec(memory_space=pltpu.HBM)
     dma = pltpu.SemaphoreType.DMA
     shape = jax.ShapeDtypeStruct
+    block = pltpu.VMEM((peers, 8, packed), f32)
+    small = pltpu.VMEM((peers, 8, CAP), f32)
     return pl.pallas_call(
         functools.partial(front_kernel, peers, domains),
         out_shape=(
@@ -354,33 +417,30 @@
             shape((3, 2, slots), f32),
             shape((2, 3, CHAIN, slots), f32),
         ),
-        in_specs=[vm, vm, vm, vm, vm, vm, sm, vm],
+        in_specs=[hbm] * len(args),
         out_specs=(vm, vm, vm),
         scratch_shapes=[
-            pltpu.VMEM((peers, 8, packed), f32),
-            pltpu.VMEM((peers, 8, packed), f32),
-            pltpu.VMEM((peers, 8, packed), f32),
-            pltpu.VMEM((peers, 8, packed), f32),
-            pltpu.VMEM((16, slots), f32),
-            pltpu.VMEM((32, slots), f32),
-            pltpu.VMEM((1, slots), f32),
+            *(pltpu.VMEM(a.shape, a.dtype) for a in args),
+            block, block, block, block,
+            pltpu.VMEM((48, slots), f32),
             pltpu.VMEM((1, slots), f32),
             pltpu.VMEM((1, slots), f32),
             pltpu.VMEM((CAP, CAP), f32),
-            pltpu.VMEM((slots, 4 * CAP), bf16),
+            pltpu.VMEM((144, 4 * CAP), f32),
+            pltpu.VMEM((chunk, 4 * CAP), bf16),
             pltpu.VMEM((4 * CAP, slots), bf16),
+            small, small, small, small, small,
             pltpu.VMEM((4, 32, CAP), f32),
             pltpu.VMEM((4, 32, CAP), f32),
-            pltpu.VMEM((4, 16, CAP), f32),
-            pltpu.VMEM((4, 16, CAP), f32),
-            dma((peers,)), dma((peers,)), dma((peers,)), dma((peers,)),
-            dma((4,)), dma((4,)), dma((4,)), dma((4,)),
-            dma((2, halo_parts)), dma((2, halo_parts)),
+            dma((len(args),)),
+            *(dma((peers,)) for _ in range(8)),
+            dma((4,)), dma((4,)),
+            dma((2, peers)), dma((2, peers)),
         ],
         compiler_params=pltpu.CompilerParams(
             collective_id=0, has_side_effects=True, vmem_limit_bytes=48 * 2**20),
         name="front",
-    )(pos, mom, thermo, types, masses, rows, count, bigm)
+    )(*args)
 
 
 def force_kernel(
@@ -540,7 +600,7 @@
     ext, moved, thermo = front(
         peers, domains, positions.transpose(1, 0, 2), momenta.transpose(1, 0, 2),
         thermostat.transpose(0, 2, 1, 3), atom_types.reshape(1, slots),
-        masses.reshape(1, -1), move_rows[0], move_count, jnp.asarray(cycle_map(peers)))
+        masses.reshape(1, -1), move_rows[0], move_count)
     forces, momenta_out, positions_out, kinds, thermo_out = pair_forces(
         tile_pairs[0], tile_count, ext, moved, thermo, pair_table)
     return (

time: 79.6 us -> 78.6 us (0.987)
  the two profiles are of different devices: /device:TPU:4 before, /device:TPU:6 now
where the time goes in v3:
time: 78.6 us; the launch traced here: 78.2 us
  Pallas kernels  70.8 us (90%)
  local copies, waits for them, and re-layouts  6.11 us (8%)
  between operations  1.34 us (2%)
    pallas_call x1, Pallas kernels, front(): pl.pallas_call(functools.partial(front_kernel, peers, domains), out_shape...  36.7 us
    pallas_call x1, Pallas kernels, pair_forces(): pl.pallas_call(force_kernel, out_shape=(beads, beads, beads, shape((1, sl...  34.1 us
    unnamed x22, local copies, waits for them, and re-layouts  6.11 us

profile of v3, /device:TPU:6, one launch (start us, length us, event | category | flops | bytes accessed | tf_op | source)
XLA Modules:
  0.0 78.2 jit_solution(9989830974003895260)
XLA Ops:
  1.3 0.0 copy-start.8
  1.3 0.0 copy-start.9
  1.3 0.0 copy-start.10
  1.3 0.7 copy-done.8
  2.0 0.0 copy-done.9
  2.0 0.0 copy-done.10
  2.0 0.0 copy-start
  2.0 1.1 %copy-done = f32[2,4,3,6144]{3,1,2,0:T(4,128)S(1)} copy-done((f32[2,4,3,6144]{3,1,2,0:T(4,128)S(1)}, f32[2,4,3,6144]{3,1,2,0:T(4,128)}, u32[]{:S(2)}) %copy-start) | copy-done | bytes 589848
  3.0 0.0 copy-start.1
  3.0 0.9 %copy-done.1 = f32[192,192]{1,0:T(8,128)S(1)} copy-done((f32[192,192]{1,0:T(8,128)S(1)}, f32[192,192]{1,0:T(8,128)}, u32[]{:S(2)}) %copy-start.1) | copy-done | bytes 147480
  4.0 0.0 copy-start.2
  4.0 0.9 %copy-done.2 = f32[2,3,6144]{2,0,1:T(2,128)S(1)} copy-done((f32[2,3,6144]{2,0,1:T(2,128)S(1)}, f32[2,3,6144]{2,0,1:T(2,128)}, u32[]{:S(2)}) %copy-start.2) | copy-done | bytes 147480
  4.9 0.0 copy-start.3
  4.9 0.9 %copy-done.3 = f32[2,3,6144]{2,0,1:T(2,128)S(1)} copy-done((f32[2,3,6144]{2,0,1:T(2,128)S(1)}, f32[2,3,6144]{2,0,1:T(2,128)}, u32[]{:S(2)}) %copy-start.3) | copy-done | bytes 147480
  5.8 0.0 copy-start.4
  5.8 0.9 %copy-done.4 = f32[192,64]{1,0:T(8,128)S(1)} copy-done((f32[192,64]{1,0:T(8,128)S(1)}, f32[192,64]{1,0:T(8,128)}, u32[]{:S(2)}) %copy-start.4) | copy-done | bytes 49176
  6.7 0.0 copy-start.6
  6.7 0.7 copy-done.6
  7.4 0.0 copy-start.5
  7.4 0.0 copy-start.7
  7.4 36.7 %front.1 = (f32[3,8,6144]{2,1,0:T(8,128)S(1)}, f32[3,2,6144]{2,1,0:T(2,128)S(1)}, f32[2,3,4,6144]{3,2,1,0:T(4,128)S(1)}) custom-call(f32[3,2,6144]{2,1,0:T(2,128)S(1)} %bitcast.13, f32[3,2,6144]{2,1,0:T(2,128)S(1)} %bitcast.14, f32[2,3,4,6144]{3,2,1,0:T(4,128)S(1)} %bitcast.12, s32[1,6144]{1,0:T(1,128)S(1)} %bitcast.15, f32[1,128]{1,0:T(1,128)S(1)} %bitcast.18, ...), custom_call_target="tpu_custom_call" | custom-call | tf_op jit(solution)/shard_map/front/pallas_call | solution.py:413
  44.1 0.0 copy-done.5
  44.1 0.0 copy-done.7
  44.1 34.1 %pair_forces.1 = (f32[3,2,6144]{2,1,0:T(2,128)}, f32[3,2,6144]{2,1,0:T(2,128)}, f32[3,2,6144]{2,1,0:T(2,128)}, s32[1,6144]{1,0:T(1,128)}, f32[2,3,4,6144]{3,2,1,0:T(4,128)}) custom-call(s32[2,672]{1,0:T(2,128)S(1)} %bitcast.16, s32[1]{0:T(128)S(6)} %copy.17.count, f32[3,8,6144]{2,1,0:T(8,128)S(1)} %get-tuple-element.13.ext, ...), custom_call_target="tpu_custom_call" | custom-call | tf_op jit(solution)/shard_map/pair_forces/pallas_call | solution.py:577
Async XLA Ops:
  1.3 0.7 copy-start.8
  1.3 0.7 copy-start.9
  1.3 0.7 copy-start.10
  2.0 1.1 %copy-start = (f32[2,4,3,6144]{3,1,2,0:T(4,128)S(1)}, f32[2,4,3,6144]{3,1,2,0:T(4,128)}, u32[]{:S(2)}) copy-start(f32[2,4,3,6144]{3,1,2,0:T(4,128)} %param.14) | copy-start | bytes 1769476
  3.0 0.9 %copy-start.1 = (f32[192,192]{1,0:T(8,128)S(1)}, f32[192,192]{1,0:T(8,128)}, u32[]{:S(2)}) copy-start(f32[192,192]{1,0:T(8,128)} %constant.4.clone.big_in) | copy-start | bytes 442372
  4.0 0.9 %copy-start.2 = (f32[2,3,6144]{2,0,1:T(2,128)S(1)}, f32[2,3,6144]{2,0,1:T(2,128)}, u32[]{:S(2)}) copy-start(f32[2,3,6144]{2,0,1:T(2,128)} %param.12) | copy-start | bytes 442372
  4.9 0.9 %copy-start.3 = (f32[2,3,6144]{2,0,1:T(2,128)S(1)}, f32[2,3,6144]{2,0,1:T(2,128)}, u32[]{:S(2)}) copy-start(f32[2,3,6144]{2,0,1:T(2,128)} %param.13) | copy-start | bytes 442372
  5.8 0.9 %copy-start.4 = (f32[192,64]{1,0:T(8,128)S(1)}, f32[192,64]{1,0:T(8,128)}, u32[]{:S(2)}) copy-start(f32[192,64]{1,0:T(8,128)} %constant.5.clone.small_in) | copy-start | bytes 147460
  6.7 0.7 copy-start.6
  7.4 36.7 %copy-start.5 = (bf16[128,128]{1,0:T(8,128)(2,1)S(1)}, bf16[128,128]{1,0:T(8,128)(2,1)}, u32[]{:S(2)}) copy-start(bf16[128,128]{1,0:T(8,128)(2,1)} %table.1) | copy-start | bytes 98308
  7.4 36.7 %copy-start.7 = (s32[1,2,672]{2,1,0:T(2,128)S(1)}, s32[1,2,672]{2,1,0:T(2,128)}, u32[]{:S(2)}) copy-start(s32[1,2,672]{2,1,0:T(2,128)} %param.18) | copy-start | bytes 16132

commit v4 on v3

--- a/solution.py
+++ b/solution.py
@@ -82,11 +82,11 @@
 def front_kernel(
     peers, domains,
     pos_in, mom_in, thermo_in, types_in, masses_in, rows_in, count_in, big_in, small_in,
-    ext, momo, tho,
+    ext_out, momo_out, tho_out,
     pos, mom, thermo, types, masses, rows, count, bigm, smallm,
     send1, recv1, send2, recv2, pth, mass, mask, into, picked, gat, sca,
-    mig1, got1, mig2, got2, scale, e_out, e_in,
-    load, s1, r1, s2, r2, sm1, rm1, sm2, rm2, se, re, sh, rh,
+    mig1, got1, mig2, got2, scale, e_out, e_in, ext, momo, tho,
+    load, save, s1, r1, s2, r2, sm1, rm1, sm2, rm2, se, re, sh, rh,
 ):
     slots = pos.shape[2]
     chunk = slots // peers
@@ -327,11 +327,13 @@
                 for link in range(CHAIN):
                     row = 6 * link + 2 * n + bead
                     tho[bead, n, link : link + 1, at] = merged[row : row + 1]
-        ext[1, 6:7, at] = jnp.where(hit > 0.5, new[72:73], pth[24:25, at])
-        return carry
-
-    ext[1, 7:8] = jnp.zeros((1, slots), f32)
+        ext[6:7, at] = jnp.where(hit > 0.5, new[72:73], pth[24:25, at])
+        return carry
+
+    ext[7:8] = jnp.zeros((1, slots), f32)
     lax.fori_loop(0, slots // 256, early_land, 0, unroll=2)
+    chains = pltpu.make_async_copy(tho, tho_out, load.at[0])
+    chains.start()
 
     def take_turned(q, carry):
         delivered(q).wait_recv()
@@ -347,9 +349,15 @@
     def halo(side, p, to):
         cut = lanes(p * chunk, chunk)
         return pltpu.make_async_remote_copy(
-            src_ref=ext.at[1, :, cut], dst_ref=ext.at[2 * side, :, cut],
+            src_ref=ext.at[:, cut], dst_ref=ext_out.at[2 * side, :, cut],
             send_sem=sh.at[side, p], recv_sem=rh.at[side, p],
             device_id=(me_b, domain(to)), device_id_type=MESH)
+
+    def keep(p):
+        cut = lanes(p * chunk, chunk)
+        return (
+            pltpu.make_async_copy(ext.at[:, cut], ext_out.at[1, :, cut], save.at[0, p]),
+            pltpu.make_async_copy(momo.at[:, :, cut], momo_out.at[:, :, cut], save.at[1, p]))
 
     def merge(p):
         at = lanes(p * chunk, chunk)
@@ -359,13 +367,15 @@
         m = mass[:, at]
         main = recv2[p, :, 0:chunk]
         rest = recv2[p, :, chunk : chunk + half]
-        ext[1, 0:6, at] = jnp.where(hit, new[0:6], main[0:6])
+        ext[0:6, at] = jnp.where(hit, new[0:6], main[0:6])
         halo(0, p, 1).start()
         halo(1, p, -1).start()
         drift = jnp.concatenate([main[6:8], jnp.concatenate([rest[0:4], rest[4:8]], axis=1)], axis=0)
         drift = jnp.where(hit, new[8:14], drift * m)
         for n in range(3):
             momo[n, :, at] = drift[2 * n : 2 * n + 2]
+        for copy in keep(p):
+            copy.start()
 
     merge(me_b)
 
@@ -393,9 +403,12 @@
         halo(1, p, -1).wait_send()
         halo(0, p, -1).wait_recv()
         halo(1, p, 1).wait_recv()
+        for copy in keep(p):
+            copy.wait()
         return carry
 
     lax.fori_loop(0, peers, take_halo, 0)
+    chains.wait()
 
 
 def front(peers, domains, pos, mom, thermo, types, masses, rows, count):
@@ -404,7 +417,6 @@
     packed = chunk + chunk // 2
     bigm, smallm = (jnp.asarray(m) for m in cycle_map(peers))
     args = (pos, mom, thermo, types, masses, rows, count, bigm, smallm)
-    vm = pl.BlockSpec(memory_space=pltpu.VMEM)
     hbm = pl.BlockSpec(memory_space=pltpu.HBM)
     dma = pltpu.SemaphoreType.DMA
     shape = jax.ShapeDtypeStruct
@@ -418,7 +430,7 @@
             shape((2, 3, CHAIN, slots), f32),
         ),
         in_specs=[hbm] * len(args),
-        out_specs=(vm, vm, vm),
+        out_specs=(hbm, hbm, hbm),
         scratch_shapes=[
             *(pltpu.VMEM(a.shape, a.dtype) for a in args),
             block, block, block, block,
@@ -432,26 +444,37 @@
             small, small, small, small, small,
             pltpu.VMEM((4, 32, CAP), f32),
             pltpu.VMEM((4, 32, CAP), f32),
-            dma((len(args),)),
+            pltpu.VMEM((8, slots), f32),
+            pltpu.VMEM((3, 2, slots), f32),
+            pltpu.VMEM((2, 3, CHAIN, slots), f32),
+            dma((len(args),)), dma((2, peers)),
             *(dma((peers,)) for _ in range(8)),
             dma((4,)), dma((4,)),
             dma((2, peers)), dma((2, peers)),
         ],
         compiler_params=pltpu.CompilerParams(
-            collective_id=0, has_side_effects=True, vmem_limit_bytes=48 * 2**20),
+            collective_id=0, has_side_effects=True, vmem_limit_bytes=56 * 2**20),
         name="front",
     )(*args)
 
 
 def force_kernel(
-    tiles, count, ext, mom, thermo, table,
-    force, momo, poso, kindo, tho,
-    far, near, strength, moment, total, w0, w1, sem,
+    tiles, count, ext_in, mom_in, thermo, table,
+    force_out, momo_out, poso_out, kindo_out, tho,
+    far, near, strength, moment, total, w0, w1, ext, mom, force, momo, poso, kindo, sem,
 ):
     slots = ext.shape[2]
     cells = slots // CAP
-    keep = pltpu.make_async_copy(thermo, tho, sem)
+    take = [pltpu.make_async_copy(ext_in.at[d], ext.at[d], sem.at[d]) for d in (1, 0, 2)]
+    take.append(pltpu.make_async_copy(mom_in, mom, sem.at[3]))
+    keep = pltpu.make_async_copy(thermo, tho, sem.at[4])
+    for copy in take:
+        copy.start()
     keep.start()
+    give = [
+        pltpu.make_async_copy(src, dst, sem.at[5 + n])
+        for n, (src, dst) in enumerate(
+            [(poso, poso_out), (kindo, kindo_out), (force, force_out), (momo, momo_out)])]
     rid = lax.broadcasted_iota(jnp.int32, (8, CAP), 0)
     comp = rid // 2
     parity = lax.rem(rid, 2)
@@ -486,11 +509,15 @@
 
         lax.fori_loop(0, cells, body, 0, unroll=prep_unroll)
 
-    for dom in range(3):
-        prepare_far(dom)
+    take[0].wait()
+    prepare_far(1)
 
     def prepare_near(c, carry):
         block, x = scaled(1, c, log_scale)
+        at = cell_at(c)
+        for n in range(3):
+            poso[n, :, at] = block[2 * n : 2 * n + 2]
+        kindo[:, at] = block[6:7].astype(jnp.int32)
         x1, x2, x3 = split3(x)
         kind = jnp.broadcast_to(block[6:7], (CAP, CAP))
         onehot = jnp.where(kind == subl, 1.0, 0.0).astype(bf16)
@@ -506,6 +533,12 @@
         return carry
 
     lax.fori_loop(0, cells, prepare_near, 0, unroll=prep_unroll)
+    give[0].start()
+    give[1].start()
+    for copy in take[1:]:
+        copy.wait()
+    prepare_far(0)
+    prepare_far(2)
     near[cells] = jnp.zeros(near.shape[1:], bf16)
     strength[cells] = jnp.zeros(strength.shape[1:], bf16)
     total[...] = jnp.zeros(total.shape, f32)
@@ -558,12 +591,14 @@
             pair = got[2 * n : 2 * n + 2]
             force[n, :, at] = pair
             momo[n, :, at] = mom[n, :, at] + inner_step * pair
-            poso[n, :, at] = block[2 * n : 2 * n + 2]
-        kindo[:, at] = block[6:7].astype(jnp.int32)
         return carry
 
     lax.fori_loop(0, cells, finish, 0, unroll=prep_unroll)
+    give[2].start()
+    give[3].start()
     keep.wait()
+    for copy in give:
+        copy.wait()
 
 
 def pair_forces(tiles, count, ext, mom, thermo, table):
@@ -571,14 +606,14 @@
     cells = slots // CAP
     vm = pl.BlockSpec(memory_space=pltpu.VMEM)
     sm = pl.BlockSpec(memory_space=pltpu.SMEM)
-    hbm = pl.BlockSpec(memory_space=pl.ANY)
+    hbm = pl.BlockSpec(memory_space=pltpu.HBM)
     shape = jax.ShapeDtypeStruct
     beads = shape((3, 2, slots), f32)
     return pl.pallas_call(
         force_kernel,
         out_shape=(beads, beads, beads, shape((1, slots), jnp.int32), shape(thermo.shape, f32)),
-        in_specs=[sm, sm, vm, vm, hbm, vm],
-        out_specs=(vm, vm, vm, vm, hbm),
+        in_specs=[sm, sm, hbm, hbm, hbm, vm],
+        out_specs=(hbm,) * 5,
         scratch_shapes=[
             pltpu.VMEM((3 * cells, CAP, 256), bf16),
             pltpu.VMEM((cells + 1, 48, 256), bf16),
@@ -587,9 +622,12 @@
             pltpu.VMEM((cells + 1, 8, CAP), f32),
             pltpu.VMEM((batch, 256, 256), bf16),
             pltpu.VMEM((batch, 256, 256), bf16),
-            pltpu.SemaphoreType.DMA,
+            pltpu.VMEM((3, 8, slots), f32),
+            *(pltpu.VMEM((3, 2, slots), f32) for _ in range(4)),
+            pltpu.VMEM((1, slots), jnp.int32),
+            pltpu.SemaphoreType.DMA((9,)),
         ],
-        compiler_params=pltpu.CompilerParams(vmem_limit_bytes=48 * 2**20),
+        compiler_params=pltpu.CompilerParams(vmem_limit_bytes=56 * 2**20),
         name="pair_forces",
     )(tiles, count, ext, mom, thermo, table)
 

time: 78.6 us -> 71.7 us (0.912)
  the two profiles are of different devices: /device:TPU:6 before, /device:TPU:15 now
where the time goes in v4:
time: 71.7 us; the launch traced here: 71.5 us
  Pallas kernels  70.2 us (98%)
  between operations  1.29 us (2%)
    pallas_call x1, Pallas kernels, front(): pl.pallas_call(functools.partial(front_kernel, peers, domains), out_shape...  35.3 us
    pallas_call x1, Pallas kernels, pair_forces(): pl.pallas_call(force_kernel, out_shape=(beads, beads, beads, shape((1, sl...  34.9 us

profile of v4, /device:TPU:15, one launch (start us, length us, event | category | flops | bytes accessed | tf_op | source)
XLA Modules:
  0.0 71.5 jit_solution(2937555185386027972)
XLA Ops:
  1.3 35.3 %front.1 = (f32[3,8,6144]{2,1,0:T(8,128)}, f32[3,2,6144]{2,1,0:T(2,128)}, f32[2,3,4,6144]{3,2,1,0:T(4,128)}) custom-call(f32[3,2,6144]{2,1,0:T(2,128)} %bitcast.13, f32[3,2,6144]{2,1,0:T(2,128)} %bitcast.14, f32[2,3,4,6144]{3,2,1,0:T(4,128)} %bitcast.12, s32[1,6144]{1,0:T(1,128)} %bitcast.15, f32[1,128]{1,0:T(1,128)} %bitcast.18, s32[4,96]{1,0:T(4,128)} %bitcast.17, ...), custom_call_target="tpu_custom_call" | custom-call | tf_op jit(solution)/shard_map/front/pallas_call | solution.py:425
  36.6 34.9 %pair_forces.1 = (f32[3,2,6144]{2,1,0:T(2,128)}, f32[3,2,6144]{2,1,0:T(2,128)}, f32[3,2,6144]{2,1,0:T(2,128)}, s32[1,6144]{1,0:T(1,128)}, f32[2,3,4,6144]{3,2,1,0:T(4,128)}) custom-call(s32[2,672]{1,0:T(2,128)} %bitcast.16, s32[1]{0:T(128)S(6)} %copy.17.count, f32[3,8,6144]{2,1,0:T(8,128)} %get-tuple-element.13.ext_in, ...), custom_call_target="tpu_custom_call" | custom-call | tf_op jit(solution)/shard_map/pair_forces/pallas_call | solution.py:612

commit v5 on v4

--- a/solution.py
+++ b/solution.py
@@ -29,7 +29,7 @@
 spread = math.sqrt(1.0 / (reach2 * math.log(2.0)))
 log_scale = math.log2(1.0 / (reach2 * NBEADS))
 centre = (0.5, 4.0, 3.0)
-batch = 16
+batch = 24
 prep_unroll = 16
 
 
@@ -206,14 +206,15 @@
         into[8 + c : 9 + c] = jnp.where(live, listed[other : other + 1], -1.0)
     landing = into[...].T
     picked[...] = jnp.zeros(picked.shape, f32)
-    row_iota = lax.broadcasted_iota(jnp.int32, (CAP, CAP), 0)
+    row_iota = lax.broadcasted_iota(jnp.int32, (CAP, CAP), 0).astype(f32).astype(bf16)
+    one, zero = jnp.ones((CAP, CAP), bf16), jnp.zeros((CAP, CAP), bf16)
 
     def pick(n, carry):
         for k in range(chunk // CAP):
-            slot = (row_iota + (n * chunk + k * CAP)).astype(f32)
+            local = (listed - (n * chunk + k * CAP).astype(f32)).astype(bf16)
             for c in range(4):
                 gat[k * CAP : (k + 1) * CAP, c * CAP : (c + 1) * CAP] = jnp.where(
-                    slot == listed[c : c + 1], 1.0, 0.0).astype(bf16)
+                    row_iota == jnp.broadcast_to(local[c : c + 1], (CAP, CAP)), one, zero)
         left = jnp.concatenate(split3(pth[:, lanes(n * chunk, chunk)]), axis=0).astype(bf16)
         picked[...] += jnp.dot(left, gat[...], preferred_element_type=f32)
         return carry
@@ -249,15 +250,6 @@
     for c in range(4):
         e_out[c] = leaving[0:32, c * CAP : (c + 1) * CAP]
         hop(e_out, e_in, se, re, c, offsets[c]).start()
-
-    def land_map(n, carry):
-        at = lanes(n * CAP, CAP)
-        slot = (lax.broadcasted_iota(jnp.int32, (CAP, CAP), 1) + n * CAP).astype(f32)
-        for c in range(4):
-            sca[c * CAP : (c + 1) * CAP, at] = jnp.where(slot == landing[:, 8 + c : 9 + c], 1.0, 0.0).astype(bf16)
-        return carry
-
-    lax.fori_loop(0, slots // CAP, land_map, 0, unroll=2)
 
     def take1(off, carry):
         arrival(send1, recv1, s1, r1, off).wait_recv()
@@ -307,6 +299,19 @@
     lax.fori_loop(0, peers, send_turned, 0)
     lax.fori_loop(0, peers - 1, send_mixed, 0)
     recv2[me_b] = send2[me_b]
+
+    landed = [jnp.broadcast_to(landing[:, 8 + c : 9 + c], (CAP, CAP)) for c in range(4)]
+    lane_iota = lax.broadcasted_iota(jnp.int32, (CAP, CAP), 1).astype(f32).astype(bf16)
+
+    def land_map(n, carry):
+        at = lanes(n * CAP, CAP)
+        for c in range(4):
+            local = (landed[c] - (n * CAP).astype(f32)).astype(bf16)
+            sca[c * CAP : (c + 1) * CAP, at] = jnp.where(lane_iota == local, one, zero)
+        return carry
+
+    lax.fori_loop(0, slots // CAP, land_map, 0, unroll=2)
+
 
     for c in range(4):
         hop(e_out, e_in, se, re, c, -offsets[c]).wait_recv()

time: 71.7 us -> 69.9 us (0.975)
  the two profiles are of different devices: /device:TPU:15 before, /device:TPU:5 now
where the time goes in v5:
time: 69.9 us; the launch traced here: 69.7 us
  Pallas kernels  68.4 us (98%)
  between operations  1.29 us (2%)
    pallas_call x1, Pallas kernels, front(): pl.pallas_call(functools.partial(front_kernel, peers, domains), out_shape...  34.5 us
    pallas_call x1, Pallas kernels, pair_forces(): pl.pallas_call(force_kernel, out_shape=(beads, beads, beads, shape((1, sl...  34 us

profile of v5, /device:TPU:5, one launch (start us, length us, event | category | flops | bytes accessed | tf_op | source)
XLA Modules:
  0.0 69.7 jit_solution(12501115528743510517)
XLA Ops:
  1.3 34.5 %front.1 = (f32[3,8,6144]{2,1,0:T(8,128)}, f32[3,2,6144]{2,1,0:T(2,128)}, f32[2,3,4,6144]{3,2,1,0:T(4,128)}) custom-call(f32[3,2,6144]{2,1,0:T(2,128)} %bitcast.13, f32[3,2,6144]{2,1,0:T(2,128)} %bitcast.14, f32[2,3,4,6144]{3,2,1,0:T(4,128)} %bitcast.12, s32[1,6144]{1,0:T(1,128)} %bitcast.15, f32[1,128]{1,0:T(1,128)} %bitcast.18, s32[4,96]{1,0:T(4,128)} %bitcast.17, ...), custom_call_target="tpu_custom_call" | custom-call | tf_op jit(solution)/shard_map/front/pallas_call | solution.py:430
  35.8 34.0 %pair_forces.1 = (f32[3,2,6144]{2,1,0:T(2,128)}, f32[3,2,6144]{2,1,0:T(2,128)}, f32[3,2,6144]{2,1,0:T(2,128)}, s32[1,6144]{1,0:T(1,128)}, f32[2,3,4,6144]{3,2,1,0:T(4,128)}) custom-call(s32[2,672]{1,0:T(2,128)} %bitcast.16, s32[1]{0:T(128)S(6)} %copy.17.count, f32[3,8,6144]{2,1,0:T(8,128)} %get-tuple-element.13.ext_in, ...), custom_call_target="tpu_custom_call" | custom-call | tf_op jit(solution)/shard_map/pair_forces/pallas_call | solution.py:617
